TPU v7x, 128 devices: a whole 4x4x4 slice. The times are simulated.
128 devices in a mesh: visit: 8 (over y, core), sky: 16 (over z, x).
Axes of the slice: x: 4, y: 4, z: 4, core: 2. Of those that a mesh axis runs over, the one named last changes fastest.
Arguments:
- tiles: bfloat16 [2048, 256, 256], P(('visit', 'sky')), may hold values from -6 to 6
- shift_int: int32 [2048, 2], P(('visit', 'sky')), may hold values from -3 to 3
- shift_frac: float32 [2048, 2], P(('visit', 'sky')), may hold values from 0 to 1
- tile_weight: float32 [2048], replicated, may hold values from 0.25 to 4
- tile_patch: int32 [2048], replicated, may hold values from 0 to 63, as said below
- al_coeff: float32 [2048, 10], P(('visit', 'sky')), may hold values from -3 to 3
Outputs:
- coadd: float32 [64, 256, 256], P('sky', 'visit')
- difference: float32 [2048, 256, 256], P(('visit', 'sky'))
Inputs may be any that keep to these rules, and one draw needn't show every extreme that they name: `tile_patch`: the owner of patch p is p // 4. Among the 16 tiles of one device (consecutive in the tile order) at most 2 have patches of one owner, and in every draw some owner has exactly 2 tiles from every device.
All inputs are finite; a program needn't handle non-finite values.
Results may differ from a plain program's by a relative error of at most 0.0053.
Values may be sent and summed in bfloat16 or wider, within the bound.
A program may use at most 192 MiB of HBM per device.

v0:
```python
import jax
import jax.numpy as jnp
import numpy as np
from jax import lax
from jax.sharding import PartitionSpec as P

KHALF = 10
CAP = 2
NBASIS = 10
PAT_SKY = 4


sigma_list = (1.0, 2.5, 5.0)
factor_list = ((0, 0), (0, 1), (0, 2), (1, 0), (1, 1), (2, 0))
basis_rows = (0, 1, 0, 2, 0, 1, 3, 4, 3, 5)
basis_cols = (0, 0, 1, 0, 2, 1, 3, 3, 4, 5)


def lanczos(shift, count):
    index = jnp.arange(count)
    offset = (index[None, None, :] - index[None, :, None]).astype(jnp.float32) - shift[
        :, None, None
    ]
    return jnp.where(jnp.abs(offset) < 3.0, jnp.sinc(offset) * jnp.sinc(offset / 3.0), 0.0)


def factor_mats(count):
    index = jnp.arange(count)
    diffs = (index[:, None] - index[None, :]).astype(jnp.float32)
    offsets = jnp.arange(-KHALF, KHALF + 1).astype(jnp.float32)
    mats = []
    for sigma_index, power in factor_list:
        sigma = sigma_list[sigma_index]
        norm_sum = jnp.sum(jnp.exp(-offsets * offsets / (2.0 * sigma * sigma)))
        value = (
            jnp.exp(-diffs * diffs / (2.0 * sigma * sigma)) * (diffs / sigma) ** power / norm_sum
        )
        mats.append(jnp.where(jnp.abs(diffs) <= KHALF, value, 0.0))
    return jnp.stack(mats)


def mixing_table():
    table = np.zeros((NBASIS, len(factor_list), len(factor_list)), np.float32)
    for basis in range(NBASIS):
        table[basis, basis_cols[basis], basis_rows[basis]] = 1.0
    return table


def owner_ranks(patch_rows, sky_count):
    owner = patch_rows // PAT_SKY
    hits = (owner[..., None] == jnp.arange(sky_count)).astype(jnp.int32)
    before = jnp.cumsum(hits, axis=-2) - hits
    rank = jnp.sum(before * hits, axis=-1)
    return (owner, rank)


def shards(tiles, shift_int, shift_frac, tile_weight, tile_patch, al_coeff):
    sky_count = lax.axis_size("sky")
    visit_count = lax.axis_size("visit")
    visit_pos = lax.axis_index("visit")
    sky_pos = lax.axis_index("sky")
    tile_count = tiles.shape[0]
    side = tiles.shape[1]
    slot_count = sky_count * CAP
    layout = tile_patch.reshape(visit_count, sky_count, tile_count)
    visit_lists = layout[visit_pos]
    my_patch = visit_lists[sky_pos]
    my_weight = tile_weight.reshape(visit_count, sky_count, tile_count)[visit_pos, sky_pos]
    shifts = shift_int.astype(jnp.float32) + shift_frac
    row_mat = lanczos(shifts[:, 0], side).astype(jnp.bfloat16)
    col_mat = lanczos(shifts[:, 1], side).astype(jnp.bfloat16)
    rowpass = jnp.einsum("trb,tab->tra", tiles, col_mat, preferred_element_type=jnp.float32).astype(
        jnp.bfloat16
    )
    warp = jnp.einsum("tir,tra->tia", row_mat, rowpass, preferred_element_type=jnp.float32)
    weighted = (my_weight[:, None, None] * warp).astype(jnp.bfloat16)
    my_owner, my_rank = owner_ranks(my_patch, sky_count)
    my_slot = my_owner * CAP + my_rank
    outgoing = jnp.zeros((slot_count, side, side), jnp.bfloat16).at[my_slot].set(weighted)
    incoming = lax.all_to_all(outgoing, "sky", split_axis=0, concat_axis=0, tiled=True)
    src_owner, src_rank = owner_ranks(visit_lists, sky_count)
    valid = (src_owner == sky_pos).astype(jnp.float32)
    position = jnp.arange(sky_count)[:, None] * CAP + src_rank
    local_patch = visit_lists % PAT_SKY
    patch_hot = (local_patch[..., None] == jnp.arange(PAT_SKY)).astype(jnp.float32)
    slot_hot = (position[..., None] == jnp.arange(slot_count)).astype(jnp.float32)
    selector = jnp.sum(
        valid[:, :, None, None] * patch_hot[:, :, :, None] * slot_hot[:, :, None, :], axis=(0, 1)
    )
    selector_low = selector.astype(jnp.bfloat16)
    partial_value = jnp.dot(
        selector_low, incoming.reshape(slot_count, side * side), preferred_element_type=jnp.float32
    )
    partial_value = partial_value.reshape(PAT_SKY, side, side)
    patch_ids = sky_pos * PAT_SKY + jnp.arange(PAT_SKY)
    weight_sum = jnp.sum(
        jnp.where(tile_patch[None, :] == patch_ids[:, None], tile_weight[None, :], 0.0), axis=1
    )
    denominator = (1.0 + weight_sum)[:, None, None]
    summed_rows = lax.psum_scatter(partial_value, "visit", scatter_dimension=1, tiled=True)
    coadd_rows = summed_rows / denominator
    template = lax.all_gather(coadd_rows.astype(jnp.bfloat16), "visit", axis=1, tiled=True)
    factors = factor_mats(side)
    factors_low = factors.astype(jnp.bfloat16)
    factor_count = len(factor_list)
    returning = jnp.dot(
        selector_low.T, template.reshape(PAT_SKY, side * side), preferred_element_type=jnp.float32
    )
    returning = returning.astype(jnp.bfloat16).reshape(sky_count, CAP, side, side)
    filtered_all = jnp.einsum(
        "nkrb,jab->nkjra",
        lax.all_to_all(returning, "sky", split_axis=0, concat_axis=0, tiled=True),
        factors_low,
        preferred_element_type=jnp.float32,
    ).astype(jnp.bfloat16)
    filtered = filtered_all.reshape(slot_count, factor_count, side, side)[my_slot]
    coeff_grid = jnp.einsum(
        "tk,kjf->tjf", al_coeff, jnp.asarray(mixing_table()), precision=lax.Precision.HIGHEST
    )
    mixed = jnp.einsum(
        "tjf,fab->tjab", coeff_grid, factors, precision=lax.Precision.HIGHEST
    ).astype(jnp.bfloat16)
    convolved = jnp.einsum("tjir,tjra->tia", mixed, filtered, preferred_element_type=jnp.float32)
    difference = warp - convolved
    return (coadd_rows, difference)


def solution(mesh):
    return jax.shard_map(
        shards,
        mesh=mesh,
        in_specs=(
            P(("visit", "sky"), None, None),
            P(("visit", "sky"), None),
            P(("visit", "sky"), None),
            P(),
            P(),
            P(("visit", "sky"), None),
        ),
        out_specs=(P("sky", "visit", None), P(("visit", "sky"), None, None)),
        check_vma=False,
    )
```

profile of v0, /device:TPU:1, one launch (start us, length us, event | category | flops | bytes accessed | tf_op | source)
XLA Modules:
  0.0 351.5 jit_solution(6740946213181481938)
XLA Ops:
  7.2 0.0 copy-start
  7.2 0.9 reshape.400
  8.2 0.1 fusion.151
  8.3 0.2 select_reduce_fusion.1
  8.5 0.8 reshape.401
  9.3 0.7 convert_add_fusion
  10.0 0.0 copy-done
  10.0 22.0 %multiply_convert_fusion = (bf16[16,256,256]{2,1,0:T(8,128)(2,1)}, f32[16,256,256]{2,1,0:T(8,128)}) fusion(f32[16]{0:T(128)S(1)} %fusion.154, bf16[16,256,256]{2,1,0:T(8,128)(2,1)S(1)} %copy-done, f32[16]{0:T(128)S(1)} %get-tuple-element.20, f32[256,256]{1,0:T(8,128)S(1)} %subtract_convert_fusion, f32[16]{0:T(128)S(1)} %get-tuple-element.19), kind=kOutput, calls=%fused_computation.130 | convolution fusion | flops 1227882496 | bytes 8650944 | tf_op jit(solution)/shard_map/tir,tra->tia/dot_general | solution.py:75
  32.0 0.0 copy-start.2
  32.1 2.5 broadcast_in_dim.26
  34.5 0.0 copy-done.2
  34.5 5.1 %scatter_fusion = bf16[32,256,256]{2,1,0:T(8,128)(2,1)} fusion(bf16[32,256,256]{2,1,0:T(8,128)(2,1)} %broadcast_in_dim.26, s32[16]{0:T(128)S(1)} %fusion.155, bf16[16,256,256]{2,1,0:T(8,128)(2,1)S(1)} %copy-done.2), kind=kCustom, calls=%fused_computation.1 | custom fusion | bytes 6291520 | tf_op jit(solution)/shard_map/scatter | solution.py:79
  39.7 8.5 %all-to-all-start = ((bf16[32,256,256]{2,1,0:T(8,128)(2,1)}), bf16[32,256,256]{2,1,0:T(8,128)(2,1)}, u32[]{:S(2)}, u32[]{:S(2)}) async-start(bf16[32,256,256]{2,1,0:T(8,128)(2,1)} %scatter_fusion), calls=%async_computation | async-start | bytes 8388608 | tf_op jit(solution)/shard_map/all_to_all | solution.py:80
  48.2 0.0 copy-start.7
  48.2 0.0 copy-start.3
  48.2 0.0 copy-start.4
  48.2 0.2 all-reduce.3.cloned.1.call-start
  48.5 0.1 copy.29
  48.6 0.5 fusion.187
  49.0 0.1 copy.30
  49.1 0.1 fusion.146
  49.2 0.2 multiply_reduce_fusion
  49.5 61.1 %all-to-all-done = bf16[32,256,256]{2,1,0:T(8,128)(2,1)} async-done(((bf16[32,256,256]{2,1,0:T(8,128)(2,1)}), bf16[32,256,256]{2,1,0:T(8,128)(2,1)}, u32[]{:S(2)}, u32[]{:S(2)}) %all-to-all-start) | async-done | bytes 4194336 | tf_op jit(solution)/shard_map/all_to_all | solution.py:80
  110.5 5.6 %fusion.84 = f32[4,256,256]{2,0,1:T(4,128)} fusion(bf16[4,32]{1,0:T(4,128)(2,1)S(1)} %multiply_reduce_fusion, bf16[4,8,256,256]{3,2,1,0:T(8,128)(2,1)} %bitcast.30), kind=kOutput, calls=%fused_computation.109 | convolution fusion | flops 16777216 | bytes 5243136 | tf_op jit(solution)/shard_map/dot_general | solution.py:91
  116.1 0.0 all-reduce.3.cloned.1.call-update
  116.1 0.0 copy-done.7
  116.1 0.6 dynamic-slice.2
  117.4 0.0 copy-done.3
  117.4 0.0 copy-done.4
  117.4 0.2 select_reduce_fusion
  117.6 59.3 %all-reduce.3.cloned.1.call-done = f32[4,256,256]{2,0,1:T(4,128)} async-done(((f32[4,256,256]{2,0,1:T(4,128)}), f32[4,256,256]{2,0,1:T(4,128)}) %all-reduce.3.cloned.1.call-update) | async-done | bytes 1048592
  176.9 1.0 fusion.184
  178.0 15.6 %all_gather.3 = bf16[4,256,256]{2,0,1:T(4,128)(2,1)S(1)} all-gather(bf16[4,32,256]{2,0,1:T(4,128)(2,1)S(1)} %get-tuple-element.13), channel_id=1, replica_groups=mesh['visit'=8,'sky'=16] {'visit'}, dimensions={1}, use_global_device_ids=true | all-gather | bytes 589824 | tf_op jit(solution)/shard_map/all_gather | solution.py:102
  193.6 1.3 convolution_convert_fusion
  194.9 3.0 copy.41
  197.9 0.0 copy-start.5
  197.9 0.0 copy-start.6
  197.9 6.8 %all-to-all-start.1 = ((bf16[16,2,256,256]{3,2,1,0:T(8,128)(2,1)}), bf16[16,2,256,256]{3,2,1,0:T(8,128)(2,1)}, u32[]{:S(2)}, u32[]{:S(2)}) async-start(bf16[16,2,256,256]{3,2,1,0:T(8,128)(2,1)} %bitcast.103), calls=%async_computation.1 | async-start | bytes 8388608 | tf_op jit(solution)/shard_map/all_to_all | solution.py:112
  204.8 0.6 exponential_reduce_fusion.2
  205.4 0.7 exponential_reduce_fusion.1
  206.1 0.6 exponential_reduce_fusion
  206.7 0.0 copy-done.5
  206.7 0.0 copy-done.6
  206.7 0.2 convolution_bitcast_fusion
  206.9 0.8 select_dynamic-update-slice_fusion.5
  207.7 0.8 select_dynamic-update-slice_fusion.4
  208.4 0.8 select_dynamic-update-slice_fusion.3
  209.2 0.8 select_dynamic-update-slice_fusion.2
  210.0 0.8 select_dynamic-update-slice_fusion.1
  210.8 0.7 select_dynamic-update-slice_fusion
  211.5 23.5 %convolution_convert_fusion.2 = bf16[16,6,256,256]{3,0,2,1:T(8,128)(2,1)} fusion(f32[16,6,6,1]{0,2,3,1:T(8,128)S(1)} %convolution_bitcast_fusion, f32[6,256,256]{2,1,0:T(8,128)S(1)} %select_dynamic-update-slice_fusion), kind=kOutput, calls=%fused_computation.40 | convolution fusion | flops 459276288 | bytes 14158080 | tf_op jit(solution)/shard_map/tjf,fab->tjab/dot_general | solution.py:120
  235.0 0.7 copy.35
  235.7 32.2 %all-to-all-done.1 = bf16[16,2,256,256]{3,2,1,0:T(8,128)(2,1)} async-done(((bf16[16,2,256,256]{3,2,1,0:T(8,128)(2,1)}), bf16[16,2,256,256]{3,2,1,0:T(8,128)(2,1)}, u32[]{:S(2)}, u32[]{:S(2)}) %all-to-all-start.1) | async-done | bytes 4194336 | tf_op jit(solution)/shard_map/all_to_all | solution.py:112
  267.9 13.4 %convolution_convert_fusion.1 = bf16[6,256,16,2,256]{4,1,3,2,0:T(8,128)(2,1)} fusion(bf16[16,2,256,256]{3,2,1,0:T(8,128)(2,1)} %all-to-all-done.1, f32[6,256,256]{2,1,0:T(8,128)S(1)} %select_dynamic-update-slice_fusion), kind=kOutput, calls=%fused_computation.3 | convolution fusion | flops 6455427072 | bytes 30932992 | tf_op jit(solution)/shard_map/nkrb,jab->nkjra/dot_general | solution.py:110
  281.3 32.6 %copy.33 = bf16[32,6,256,256]{3,2,1,0:T(8,128)(2,1)} copy(bf16[32,6,256,256]{2,3,0,1:T(8,128)(2,1)} %bitcast.101) | data formatting | bytes 50331648 | tf_op jit(solution)/shard_map/reshape | solution.py:116
  313.9 14.7 %gather_fusion = bf16[16,6,256,256]{3,2,1,0:T(8,128)(2,1)} fusion(bf16[32,6,256,256]{3,2,1,0:T(8,128)(2,1)} %copy.33, s32[1024]{0:T(1024)S(1)} %pad_clamp_fusion), kind=kCustom, calls=%fused_computation | custom fusion | bytes 25165888 | tf_op jit(solution)/shard_map/gather | solution.py:116
  328.6 0.0 copy-start.1
  328.6 16.1 %bitcast_subtract_fusion = f32[16,256,256]{2,1,0:T(8,128)} fusion(f32[16,256,256]{2,1,0:T(8,128)} %get-tuple-element.22, bf16[16,6,256,256]{3,2,1,0:T(8,128)(2,1)} %gather_fusion, bf16[16,6,256,256]{3,0,2,1:T(8,128)(2,1)} %convolution_convert_fusion.2), kind=kOutput, calls=%fused_computation.112 | convolution fusion | flops 3222274048 | bytes 33554432 | tf_op jit(solution)/shard_map/tjir,tjra->tia/dot_general | solution.py:123
  344.6 0.0 copy-done.1
  (14 shorter events, 0.2 us)
Async XLA Ops:
  7.2 2.8 copy-start
  32.0 2.5 copy-start.2
  39.7 70.8 %all-to-all-start = ((bf16[32,256,256]{2,1,0:T(8,128)(2,1)}), bf16[32,256,256]{2,1,0:T(8,128)(2,1)}, u32[]{:S(2)}, u32[]{:S(2)}) async-start(bf16[32,256,256]{2,1,0:T(8,128)(2,1)} %scatter_fusion), calls=%async_computation | async-start | bytes 8388608 | tf_op jit(solution)/shard_map/all_to_all | solution.py:80
  48.2 68.0 %copy-start.7 = (u32[128]{0:T(128)S(1)}, u32[128]{0:T(128)}, u32[]{:S(2)}) copy-start(u32[128]{0:T(128)} %constant.152) | copy-start | bytes 1540
  48.2 69.2 %copy-start.3 = (f32[2048]{0:T(1024)S(1)}, f32[2048]{0:T(1024)}, u32[]{:S(2)}) copy-start(f32[2048]{0:T(1024)} %param.11) | copy-start | bytes 24580
  48.2 69.2 %copy-start.4 = (s32[2048]{0:T(1024)S(1)}, s32[2048]{0:T(1024)}, u32[]{:S(2)}) copy-start(s32[2048]{0:T(1024)} %param.12) | copy-start | bytes 24580
  48.2 128.7 %all-reduce.3.cloned.1.call-start = ((), (), s32[]{:S(2)}) async-start(), calls=%async_computation.2 | async-start | bytes 2097152
  197.9 8.8 %copy-start.5 = (f32[10,6,6]{0,2,1:T(8,128)S(1)}, f32[10,6,6]{0,2,1:T(8,128)}, u32[]{:S(2)}) copy-start(f32[10,6,6]{0,2,1:T(8,128)} %constant.145.clone) | copy-start | bytes 4324
  197.9 8.8 %copy-start.6 = (f32[16,10]{1,0:T(8,128)S(1)}, f32[16,10]{1,0:T(8,128)}, u32[]{:S(2)}) copy-start(f32[16,10]{1,0:T(8,128)} %param.13) | copy-start | bytes 1924
  197.9 69.9 %all-to-all-start.1 = ((bf16[16,2,256,256]{3,2,1,0:T(8,128)(2,1)}), bf16[16,2,256,256]{3,2,1,0:T(8,128)(2,1)}, u32[]{:S(2)}, u32[]{:S(2)}) async-start(bf16[16,2,256,256]{3,2,1,0:T(8,128)(2,1)} %bitcast.103), calls=%async_computation.1 | async-start | bytes 8388608 | tf_op jit(solution)/shard_map/all_to_all | solution.py:112
  328.6 16.1 %copy-start.1 = (bf16[16,256,256]{2,1,0:T(8,128)(2,1)S(1)}, bf16[16,256,256]{2,1,0:T(8,128)(2,1)}, u32[]{:S(2)}) copy-start(bf16[16,256,256]{2,1,0:T(8,128)(2,1)} %param.8) | copy-start | bytes 6291460
Sparse Core Ops, SparseCore 0:
  116.2 60.6 all-reduce.2
where the time goes:
time: 353 us; the launch traced here: 351 us
  waiting for transfers between devices  153 us (43%)
  matrix products  82.1 us (23%)
  local copies, waits for them, and re-layouts  61.1 us (17%)
  blocking collectives  15.6 us (4%)
  starting transfers between devices  15.5 us (4%)
  between operations  14.9 us (4%)
  other arithmetic  9.6 us (3%)
    all_to_all x1, waiting for transfers between devices, shards(): lax.all_to_all(outgoing, 'sky', split_axis=0, concat_axis=0, tiled=True)  61.1 us
    unnamed x2, waiting for transfers between devices  59.4 us
    reshape x1, local copies, waits for them, and re-layouts, shards(): filtered_all.reshape(slot_count, factor_count, side, side)[my_slot]  32.6 us
    all_to_all x1, waiting for transfers between devices, shards(): lax.all_to_all(returning, 'sky', split_axis=0, concat_axis=0, tiled=True)  32.2 us
    dot_general x1, matrix products, shards(): jnp.einsum('tjf,fab->tjab', coeff_grid, factors, precision=lax.Precision....  23.5 us
    dot_general x1, matrix products, shards(): jnp.einsum('tir,tra->tia', row_mat, rowpass, preferred_element_type=jnp.f...  22 us
    dot_general x1, matrix products, shards(): jnp.einsum('tjir,tjra->tia', mixed, filtered, preferred_element_type=jnp....  16.1 us
    all_gather x1, blocking collectives, shards(): lax.all_gather(coadd_rows.astype(jnp.bfloat16), 'visit', axis=1, tiled=True)  15.6 us
  transfers between devices with their start and end apart: 3, of which 3 were waited for; matrix products, arithmetic and copies ran while one was open for 9% of the time, Pallas kernels for 0%

commit v1 on v0

v1 whole, which is shorter than its diff:
```python
import functools
import math

import jax
import jax.numpy as jnp
import numpy as np
from jax import lax
from jax.experimental import pallas as pl
from jax.experimental.pallas import tpu as pltpu
from jax.sharding import PartitionSpec as P

MESH = pl.DeviceIdType.MESH
KHALF = 10
SIDE = 256
TILES_DEV = 16
SIGMAS = (1.0, 2.5, 5.0)
FACTORS = ((0, 0), (0, 1), (0, 2), (1, 0), (1, 1), (2, 0))
BASIS_ROWS = (0, 1, 0, 2, 0, 1, 3, 4, 3, 5)
BASIS_COLS = (0, 0, 1, 0, 2, 1, 3, 3, 4, 5)
NF = len(FACTORS)

UNITS = ((0, 3), (3, 6), (6, 8))
GROUPS = 2
TG = TILES_DEV // GROUPS
PG = TG // 2
RB = TG * 8


def wrapped_diff():
    diff = np.arange(128)[None, :] - np.arange(8)[:, None]
    return ((diff + 64) % 128) - 64


def factor_strips():
    diff = wrapped_diff().astype(np.float64)
    reach = np.arange(-KHALF, KHALF + 1).astype(np.float64)
    ahead, back = [], []
    for sigma_index, power in FACTORS:
        sigma = SIGMAS[sigma_index]
        norm = np.sum(np.exp(-reach * reach / (2.0 * sigma * sigma)))
        for out, u in ((ahead, diff), (back, -diff)):
            value = np.exp(-u * u / (2.0 * sigma * sigma)) * (u / sigma) ** power / norm
            out.append(np.where(np.abs(u) <= KHALF, value, 0.0))
    return np.stack(ahead).astype(np.float32), np.stack(back).astype(np.float32)


def lanczos_strips(shift):
    diff = jnp.asarray(wrapped_diff().astype(np.float32))
    offset = jnp.stack(
        [
            diff[None] - shift[:, 0, None, None],
            -diff[None] - shift[:, 1, None, None],
        ],
        axis=1,
    )
    return jnp.where(jnp.abs(offset) < 3.0, jnp.sinc(offset) * jnp.sinc(offset / 3.0), 0.0)


def toeplitz_blocks(strip):
    lane = lax.broadcasted_iota(jnp.int32, (8, 128), 1)
    rows = [strip if b == 0 else pltpu.roll(strip, 8 * b, 1) for b in range(16)]
    low = lane < 64
    zero = jnp.zeros_like(strip)
    left = [jnp.where(low, zero, rows[b]) for b in (0, 1)]
    right = [jnp.where(low, rows[b], zero) for b in (14, 15)]
    for b in (0, 1):
        rows[b] = jnp.where(low, rows[b], zero)
    for b in (14, 15):
        rows[b] = jnp.where(low, zero, rows[b])

    def pack(pair):
        return jnp.concatenate(pair, axis=0).astype(jnp.bfloat16)

    return [pack(rows[2 * i : 2 * i + 2]) for i in range(8)], pack(right), pack(left)


def write_square(strip, ref):
    diag, right, left = toeplitz_blocks(strip)
    for i in range(8):
        ref[16 * i : 16 * i + 16, 0:128] = diag[i]
        ref[128 + 16 * i : 144 + 16 * i, 128:256] = diag[i]
    ref[112:128, 128:256] = right
    ref[128:144, 0:128] = left


def kernel(
    tiles_hbm,
    patch_s,
    weight_s,
    coeff_s,
    patch_v,
    weight_v,
    strips,
    ahead,
    back,
    diff_hbm,
    coadd_out,
    tiles,
    warp,
    send1,
    recv1,
    sel,
    selt,
    asend,
    arecv,
    bsend,
    brecv,
    gath,
    send4,
    recv4,
    csend,
    crecv,
    fmat,
    mband,
    rmat,
    tbuf,
    hbuf,
    s1,
    r1,
    sa,
    ra,
    sb,
    rb,
    sgb,
    rgb,
    sga,
    rga,
    s4,
    r4,
    sc,
    rc,
    in_sem,
    own1,
    own4,
    out_sem,
):
    visit, sky = lax.axis_index("visit"), lax.axis_index("sky")
    y, c = lax.div(visit, 2), lax.rem(visit, 2)
    z, x = lax.div(sky, 4), lax.rem(sky, 4)

    def dev(y_, c_, z_, x_):
        return (y_ * 2 + c_, z_ * 4 + x_)

    ring_of = (y, z, x)
    plane_of = ((x, z), (y, x), (z, y))

    def on_ring(p, pos, core):
        return (
            dev(pos, core, z, x),
            dev(y, core, pos, x),
            dev(y, core, z, pos),
        )[p]

    def on_first(p, pos):
        return (dev(y, c, z, pos), dev(pos, c, z, x), dev(y, c, pos, x))[p]

    def on_second(p, pos):
        return (dev(y, c, pos, x), dev(y, c, z, pos), dev(pos, c, z, x))[p]

    swap = (dev(z, c, y, x), dev(x, c, z, y))
    moved = (y != z, y != x)

    def fetch(g):
        return pltpu.make_async_copy(
            tiles_hbm.at[pl.ds(g * TG, TG)], tiles.at[pl.ds(g * TG, TG)], in_sem.at[g]
        )

    for g in range(GROUPS):
        fetch(g).start()

    barrier = pltpu.get_barrier_semaphore()
    pl.semaphore_signal(barrier, inc=1, device_id=dev(y, 1 - c, z, x), device_id_type=MESH)
    for p in range(3):
        for d in range(1, 4):
            for other in (0, 1):
                pl.semaphore_signal(
                    barrier,
                    inc=1,
                    device_id=on_ring(p, lax.rem(ring_of[p] + d, 4), lax.rem(c + other, 2)),
                    device_id_type=MESH,
                )
    for i in range(2):

        @pl.when(moved[i])
        def _(i=i):
            pl.semaphore_signal(barrier, inc=1, device_id=swap[i], device_id_type=MESH)

    def clear(ref):
        ref[...] = jnp.zeros(ref.shape, ref.dtype)

    @pl.loop(0, NF)
    def _(j):
        clear(fmat.at[j])

    @pl.loop(0, 4)
    def _(j):
        clear(rmat.at[j])

    def first(p, g, k):
        lo, hi = UNITS[p]
        d, other = k // 2, k % 2
        pos, core = lax.rem(ring_of[p] + d, 4), lax.rem(c + other, 2)
        src = send1.at[g, pos * 2 + core, pl.ds(lo, hi - lo)]
        dst = recv1.at[g, k, pl.ds(lo, hi - lo)]
        if k == 0:
            return pltpu.make_async_copy(src, dst, own1.at[p, g])
        return pltpu.make_async_remote_copy(
            src_ref=src,
            dst_ref=dst,
            send_sem=s1.at[p, g, k - 1],
            recv_sem=r1.at[p, g, k - 1],
            device_id=on_ring(p, pos, core),
            device_id_type=MESH,
        )

    for g in range(GROUPS):
        fetch(g).wait()

        @pl.loop(0, PG)
        def _(pair, g=g):
            scaled = []
            for half in range(2):
                t = g * TG + pair * 2 + half
                write_square(strips[t, 0], rmat.at[2 * half])
                write_square(strips[t, 1], rmat.at[2 * half + 1])
                rowpass = jnp.dot(
                    tiles[t], rmat[2 * half + 1], preferred_element_type=jnp.float32
                ).astype(jnp.bfloat16)
                value = jnp.dot(rmat[2 * half], rowpass, preferred_element_type=jnp.float32)
                warp[t] = value
                scaled.append((weight_s[(visit * 16 + sky) * TILES_DEV + t] * value).reshape(32, 8, SIDE))
            both = jnp.concatenate(scaled, axis=1).astype(jnp.bfloat16)
            rows = pl.ds(pl.multiple_of(pair * 16, 16), 16)
            for q in range(8):
                for u in range(8):
                    send1[g, q, u, rows, :] = both[4 * q + u // 2, :, 128 * (u % 2) : 128 * (u % 2) + 128]

        if g == 0:
            pl.semaphore_wait(barrier, 19 + moved[0].astype(jnp.int32) + moved[1].astype(jnp.int32))
        for p in range(3):
            for k in range(8):
                first(p, g, k).start()

    def patch_row(p, g, k, tt):
        pos, core = lax.rem(ring_of[p] + 4 - lax.div(k, 2), 4), lax.rem(c + lax.rem(k, 2), 2)
        v, s = on_ring(p, pos, core)
        patch = patch_s[(v * 16 + s) * TILES_DEV + g * TG + tt]
        if p == 0:
            patch = ((patch >> 2) & 3) * 16 + (patch >> 4) * 4 + (patch & 3)
        return patch * 8

    lane = lax.broadcasted_iota(jnp.int32, (8, 128), 1)
    high = lax.broadcasted_iota(jnp.int32, (512, 128), 0)
    for p in range(3):

        @pl.loop(0, 8)
        def _(m, p=p):
            key = jnp.zeros((8, 128), jnp.int32)
            for tt in range(16):
                j = m * 16 + tt
                g, rest = lax.div(j, 8 * TG), lax.rem(j, 8 * TG)
                row = patch_row(p, g, lax.div(rest, TG), lax.rem(rest, TG))
                key = jnp.where((lane >> 3) == tt, row, key)
            key = key + (lane & 7)
            wide = jnp.broadcast_to(key[0:1], (512, 128))
            sel[p, :, pl.ds(pl.multiple_of(m * 128, 128), 128)] = jnp.where(
                wide == high, 1.0, 0.0
            ).astype(jnp.bfloat16)

        @pl.loop(0, 64)
        def _(m, p=p):
            rows = []
            for half in range(2):
                j = m * 2 + half
                g, rest = lax.div(j, 8 * TG), lax.rem(j, 8 * TG)
                row = patch_row(p, g, lax.div(rest, TG), lax.rem(rest, TG))
                across = lax.broadcasted_iota(jnp.int32, (8, 512), 1)
                down = lax.broadcasted_iota(jnp.int32, (8, 512), 0)
                rows.append(jnp.where(across == down + row, 1.0, 0.0))
            selt[p, pl.ds(pl.multiple_of(m * 16, 16), 16), :] = jnp.concatenate(rows, axis=0).astype(
                jnp.bfloat16
            )

    for j in range(NF):
        write_square(ahead[j], fmat.at[j])

    @pl.loop(0, TILES_DEV)
    def _(t):
        for j in range(NF):
            strip = None
            for k in range(len(BASIS_COLS)):
                if BASIS_COLS[k] == j:
                    term = coeff_s[t, k] * back[BASIS_ROWS[k]]
                    strip = term if strip is None else strip + term
            diag, right, left = toeplitz_blocks(strip)
            cols = slice(128 * j, 128 * j + 128)
            mband[t, 0:16, cols] = right
            for i in range(8):
                mband[t, 16 + 16 * i : 32 + 16 * i, cols] = diag[i]
            mband[t, 144:160, cols] = left

    def second(p, d):
        lo, hi = UNITS[p]
        pos = lax.rem(plane_of[p][0] + d, 4)
        return pltpu.make_async_remote_copy(
            src_ref=asend.at[pos, pl.ds(lo, hi - lo)],
            dst_ref=arecv.at[d - 1, pl.ds(lo, hi - lo)],
            send_sem=sa.at[p, d - 1],
            recv_sem=ra.at[p, d - 1],
            device_id=on_first(p, pos),
            device_id_type=MESH,
        )

    def third(p, d):
        lo, hi = UNITS[p]
        pos = lax.rem(plane_of[p][1] + d, 4)
        return pltpu.make_async_remote_copy(
            src_ref=bsend.at[pos, pl.ds(lo, hi - lo)],
            dst_ref=brecv.at[d - 1, pl.ds(lo, hi - lo)],
            send_sem=sb.at[p, d - 1],
            recv_sem=rb.at[p, d - 1],
            device_id=on_second(p, pos),
            device_id_type=MESH,
        )

    for p in range(3):
        lo, hi = UNITS[p]
        for g in range(GROUPS):
            first(p, g, 0).wait()
            for k in range(1, 8):
                first(p, g, k).wait_recv()
        wide = jnp.concatenate([recv1[:, :, u].reshape(1024, 128) for u in range(lo, hi)], axis=1)
        total = jnp.dot(sel[p], wide, preferred_element_type=jnp.float32).astype(jnp.bfloat16)
        for u in range(lo, hi):
            asend[:, u] = total[:, 128 * (u - lo) : 128 * (u - lo) + 128].reshape(4, 128, 128)
        for d in range(1, 4):
            second(p, d).start()

    for p in range(3):
        lo, hi = UNITS[p]
        for d in range(1, 4):
            second(p, d).wait_recv()
        total = asend[plane_of[p][0], lo:hi].astype(jnp.float32)
        for d in range(1, 4):
            total = total + arecv[d - 1, lo:hi].astype(jnp.float32)
        total = total.astype(jnp.bfloat16)
        for b in range(4):
            bsend[b, lo:hi] = total[:, 32 * b : 32 * b + 32]
        for d in range(1, 4):
            third(p, d).start()

    def fourth(p, d):
        lo, hi = UNITS[p]
        mine = gath.at[plane_of[p][0], plane_of[p][1], pl.ds(lo, hi - lo)]
        return pltpu.make_async_remote_copy(
            src_ref=mine,
            dst_ref=mine,
            send_sem=sgb.at[p, d - 1],
            recv_sem=rgb.at[p, d - 1],
            device_id=on_second(p, lax.rem(plane_of[p][1] + d, 4)),
            device_id_type=MESH,
        )

    def fifth(p, d):
        lo, hi = UNITS[p]
        mine = gath.at[plane_of[p][0], :, pl.ds(lo, hi - lo)]
        return pltpu.make_async_remote_copy(
            src_ref=mine,
            dst_ref=mine,
            send_sem=sga.at[p, d - 1],
            recv_sem=rga.at[p, d - 1],
            device_id=on_first(p, lax.rem(plane_of[p][0] + d, 4)),
            device_id_type=MESH,
        )

    def to_owner(i):
        lo, hi = UNITS[i + 1]
        return pltpu.make_async_remote_copy(
            src_ref=csend.at[pl.ds(lo, hi - lo)],
            dst_ref=crecv.at[pl.ds(lo, hi - lo)],
            send_sem=sc.at[i],
            recv_sem=rc.at[i],
            device_id=swap[i],
            device_id_type=MESH,
        )

    owner_of = (z * 4 + x, y * 4 + x, z * 4 + y)
    for p in range(3):
        lo, hi = UNITS[p]
        for d in range(1, 4):
            third(p, d).wait_recv()
        total = bsend[plane_of[p][1], lo:hi].astype(jnp.float32)
        for d in range(1, 4):
            total = total + brecv[d - 1, lo:hi].astype(jnp.float32)
        parts = []
        for k in range(4):
            hit = jnp.where(patch_v[...] == owner_of[p] * 4 + k, weight_v[...], 0.0)
            weight = jnp.sum(jnp.sum(hit, axis=0, keepdims=True), axis=1, keepdims=True)
            parts.append(total[:, 8 * k : 8 * k + 8] / (1.0 + weight)[None])
        coadd = jnp.concatenate(parts, axis=1)
        csend[lo:hi] = coadd
        gath[plane_of[p][0], plane_of[p][1], lo:hi] = coadd.astype(jnp.bfloat16)
        for d in range(1, 4):
            fourth(p, d).start()

    for i in range(2):

        @pl.when(moved[i])
        def _(i=i):
            to_owner(i).start()

    for p in range(3):
        for d in range(1, 4):
            fourth(p, d).wait_recv()
        for d in range(1, 4):
            fifth(p, d).start()

    def last(p, g, k):
        lo, hi = UNITS[p]
        d, other = k // 2, k % 2
        pos, core = lax.rem(ring_of[p] + 4 - d, 4), lax.rem(c + other, 2)
        src = send4.at[g, k, pl.ds(lo, hi - lo)]
        dst = recv4.at[g, ring_of[p] * 2 + c, pl.ds(lo, hi - lo)]
        if k == 0:
            return pltpu.make_async_copy(src, dst, own4.at[p, g])
        return pltpu.make_async_remote_copy(
            src_ref=src,
            dst_ref=dst,
            send_sem=s4.at[p, g, k - 1],
            recv_sem=r4.at[p, g, k - 1],
            device_id=on_ring(p, pos, core),
            device_id_type=MESH,
        )

    per_group = 1024 // GROUPS
    for g in range(GROUPS):
        for p in range(3):
            lo, hi = UNITS[p]
            if g == 0:
                for d in range(1, 4):
                    fifth(p, d).wait_recv()
            wide = jnp.concatenate([gath[:, :, u].reshape(512, 128) for u in range(lo, hi)], axis=1)
            picked = jnp.dot(
                selt[p, per_group * g : per_group * (g + 1), :], wide, preferred_element_type=jnp.float32
            ).astype(jnp.bfloat16)
            for u in range(lo, hi):
                send4[g, :, u] = picked[:, 128 * (u - lo) : 128 * (u - lo) + 128].reshape(8, RB, 128)
            for k in range(8):
                last(p, g, k).start()

    def leave(g, pair):
        t = g * TG + pair * 2
        return pltpu.make_async_copy(
            warp.at[pl.ds(t, 2)], diff_hbm.at[pl.ds(t, 2)], out_sem.at[g, pair]
        )

    for g in range(GROUPS):
        for p in range(3):
            last(p, g, 0).wait()
            for k in range(1, 8):
                last(p, g, k).wait_recv()

        @pl.loop(0, PG)
        def _(pair, g=g):
            rows = pl.ds(pl.multiple_of(pair * 16, 16), 16)
            for q in range(8):
                for i in range(2):
                    for b in range(2):
                        upper = recv4[g, q, 4 * i + b, rows, :].astype(jnp.float32)
                        lower = recv4[g, q, 4 * i + 2 + b, rows, :].astype(jnp.float32)
                        at = 32 * q + 16 * i
                        cols = slice(128 * b, 128 * b + 128)
                        tbuf[at : at + 16, cols] = jnp.concatenate(
                            [upper[0:8], lower[0:8]], axis=0
                        ).astype(jnp.bfloat16)
                        tbuf[SIDE + at : SIDE + at + 16, cols] = jnp.concatenate(
                            [upper[8:16], lower[8:16]], axis=0
                        ).astype(jnp.bfloat16)
            for j in range(NF):
                filtered = jnp.dot(
                    tbuf[...], fmat[j], preferred_element_type=jnp.float32
                ).astype(jnp.bfloat16)
                for i in range(4):
                    hbuf[i, 128 * j : 128 * j + 128, :] = filtered[128 * i : 128 * i + 128]
            for half in range(2):
                t = g * TG + pair * 2 + half
                top = jnp.dot(
                    mband[t, 16:160, :], hbuf[2 * half], preferred_element_type=jnp.float32
                )
                low = jnp.dot(
                    mband[t, 0:144, :], hbuf[2 * half + 1], preferred_element_type=jnp.float32
                )
                warp[t, 0:112] = warp[t, 0:112] - top[0:112]
                warp[t, 112:144] = warp[t, 112:144] - (top[112:144] + low[0:32])
                warp[t, 144:256] = warp[t, 144:256] - low[32:144]
            leave(g, pair).start()

    for i in range(2):
        lo, hi = UNITS[i + 1]

        @pl.when(moved[i])
        def _(i=i):
            to_owner(i).wait()

        @pl.when(jnp.logical_not(moved[i]))
        def _(lo=lo, hi=hi):
            crecv[lo:hi] = csend[lo:hi]

    for u in range(8):
        for k in range(4):
            held = csend if u < UNITS[0][1] else crecv
            coadd_out[k, 8 * (u // 2) : 8 * (u // 2) + 8, 128 * (u % 2) : 128 * (u % 2) + 128] = held[
                u, 8 * k : 8 * k + 8
            ]

    for p in range(3):
        for g in range(GROUPS):
            for k in range(1, 8):
                first(p, g, k).wait_send()
                last(p, g, k).wait_send()
        for d in range(1, 4):
            second(p, d).wait_send()
            third(p, d).wait_send()
            fourth(p, d).wait_send()
            fifth(p, d).wait_send()

    @pl.loop(0, PG)
    def _(pair):
        for g in range(GROUPS):
            leave(g, pair).wait()


def shards(tiles, shift_int, shift_frac, tile_weight, tile_patch, al_coeff):
    strips = lanczos_strips(shift_int.astype(jnp.float32) + shift_frac)
    ahead, back = factor_strips()
    vmem = pl.BlockSpec(memory_space=pltpu.VMEM)
    smem = pl.BlockSpec(memory_space=pltpu.SMEM)
    hbm = pl.BlockSpec(memory_space=pl.ANY)
    bf16, f32 = jnp.bfloat16, jnp.float32
    dma = pltpu.SemaphoreType.DMA
    block = (GROUPS, 8, 8, RB, 128)
    difference, coadd = pl.pallas_call(
        kernel,
        out_shape=(
            jax.ShapeDtypeStruct((TILES_DEV, SIDE, SIDE), f32),
            jax.ShapeDtypeStruct((4, 32, SIDE), f32),
        ),
        in_specs=[hbm, smem, smem, smem, vmem, vmem, vmem, vmem, vmem],
        out_specs=(hbm, vmem),
        scratch_shapes=[
            pltpu.VMEM((TILES_DEV, SIDE, SIDE), bf16),
            pltpu.VMEM((TILES_DEV, SIDE, SIDE), f32),
            pltpu.VMEM(block, bf16),
            pltpu.VMEM(block, bf16),
            pltpu.VMEM((3, 512, 1024), bf16),
            pltpu.VMEM((3, 1024, 512), bf16),
            pltpu.VMEM((4, 8, 128, 128), bf16),
            pltpu.VMEM((3, 8, 128, 128), bf16),
            pltpu.VMEM((4, 8, 32, 128), bf16),
            pltpu.VMEM((3, 8, 32, 128), bf16),
            pltpu.VMEM((4, 4, 8, 32, 128), bf16),
            pltpu.VMEM(block, bf16),
            pltpu.VMEM(block, bf16),
            pltpu.VMEM((8, 32, 128), f32),
            pltpu.VMEM((8, 32, 128), f32),
            pltpu.VMEM((NF, SIDE, SIDE), bf16),
            pltpu.VMEM((TILES_DEV, 160, 128 * NF), bf16),
            pltpu.VMEM((4, SIDE, SIDE), bf16),
            pltpu.VMEM((2 * SIDE, SIDE), bf16),
            pltpu.VMEM((4, 128 * NF, SIDE), bf16),
            dma((3, GROUPS, 7)),
            dma((3, GROUPS, 7)),
            dma((3, 3)),
            dma((3, 3)),
            dma((3, 3)),
            dma((3, 3)),
            dma((3, 3)),
            dma((3, 3)),
            dma((3, 3)),
            dma((3, 3)),
            dma((3, GROUPS, 7)),
            dma((3, GROUPS, 7)),
            dma((2,)),
            dma((2,)),
            dma((GROUPS,)),
            dma((3, GROUPS)),
            dma((3, GROUPS)),
            dma((GROUPS, PG)),
        ],
        compiler_params=pltpu.CompilerParams(
            collective_id=0, has_side_effects=True, vmem_limit_bytes=56 << 20
        ),
    )(
        tiles,
        tile_patch,
        tile_weight,
        al_coeff,
        tile_patch.reshape(16, 128),
        tile_weight.reshape(16, 128),
        strips,
        jnp.asarray(ahead),
        jnp.asarray(back),
    )
    return coadd, difference


def solution(mesh):
    return jax.shard_map(
        shards,
        mesh=mesh,
        in_specs=(
            P(("visit", "sky"), None, None),
            P(("visit", "sky"), None),
            P(("visit", "sky"), None),
            P(),
            P(),
            P(("visit", "sky"), None),
        ),
        out_specs=(P("sky", "visit", None), P(("visit", "sky"), None, None)),
        check_vma=False,
    )
```

time: 353 us -> 79.4 us (0.22)
  waiting for transfers between devices: 153 us -> 0 us
  matrix products: 82.1 us -> 0 us
  Pallas kernels: 0 us -> 69.8 us
  local copies, waits for them, and re-layouts: 61.1 us -> 6.17 us
  blocking collectives: 15.6 us -> 0 us
  starting transfers between devices: 15.5 us -> 0 us
  between operations: 14.9 us -> 0.65 us
  other arithmetic: 9.6 us -> 2.47 us
    all_to_all x2 -> x0, waiting for transfers between devices: 93.2 us -> none  [the longest x1 61.1 us: shards(): lax.all_to_all(outgoing, 'sky', split_axis=0, concat_axis=0, tiled=True)]
    dot_general x7 -> x0, matrix products: 82.1 us -> none  [the longest x1 23.5 us: shards(): jnp.einsum('tjf,fab->tjab', coeff_grid, factors, precision=lax.Precision....]
    pallas_call x0 -> x1, Pallas kernels: none -> 69.8 us  [shards(): pl.pallas_call(kernel, out_shape=(jax.ShapeDtypeStruct((TILES_DEV, SIDE,...]
    unnamed x2 -> x0, waiting for transfers between devices: 59.4 us -> none
    reshape x3 -> x0, local copies, waits for them, and re-layouts: 34.3 us -> none  [the longest x1 32.6 us: shards(): filtered_all.reshape(slot_count, factor_count, side, side)[my_slot]]
    all_gather x1 -> x0, blocking collectives: 15.6 us -> none  [shards(): lax.all_gather(coadd_rows.astype(jnp.bfloat16), 'visit', axis=1, tiled=True)]
    all_to_all x2 -> x0, starting transfers between devices: 15.3 us -> none  [the longest x1 8.48 us: shards(): lax.all_to_all(outgoing, 'sky', split_axis=0, concat_axis=0, tiled=True)]
    gather x1 -> x0, local copies, waits for them, and re-layouts: 14.7 us -> none  [shards(): filtered_all.reshape(slot_count, factor_count, side, side)[my_slot]]
  transfers between devices with their start and end apart: 3 -> 0, of which waited for: 3 -> 0; matrix products, arithmetic and copies ran while one was open for 9% -> 0% of each run, Pallas kernels for 0% -> 0%
where the time goes in v1:
time: 79.4 us; the launch traced here: 79.1 us
  Pallas kernels  69.8 us (88%)
  local copies, waits for them, and re-layouts  6.17 us (8%)
  other arithmetic  2.47 us (3%)
    pallas_call x1, Pallas kernels, shards(): pl.pallas_call(kernel, out_shape=(jax.ShapeDtypeStruct((TILES_DEV, SIDE,...  69.8 us
    unnamed x2, local copies, waits for them, and re-layouts  6.16 us

profile of v1, /device:TPU:1, one launch (start us, length us, event | category | flops | bytes accessed | tf_op | source)
XLA Modules:
  0.0 79.1 jit_solution(1415051678911851082)
XLA Ops:
  0.6 0.7 convert_add_fusion
  1.3 0.8 %broadcast_subtract_fusion = (f32[16,1,8,128]{3,2,1,0:T(8,128)S(1)}, f32[16,1,8,128]{3,2,1,0:T(8,128)S(1)}) fusion(f32[16]{0:T(128)S(1)} %get-tuple-element.8, f32[8,128]{1,0:T(8,128)} %constant.45, f32[16]{0:T(128)S(1)} %get-tuple-element.7, f32[8,128]{1,0:T(8,128)} %constant.38.clone), kind=kLoop, calls=%fused_computation.50 | loop fusion | flops 32768 | bytes 139392 | tf_op jit(solution)/shard_map/sub | solution.py:52
  2.1 1.0 %fusion.26.strips = f32[16,2,8,128]{3,2,1,0:T(8,128)} fusion(f32[16,1,8,128]{3,2,1,0:T(8,128)S(1)} %get-tuple-element.9, f32[16,1,8,128]{3,2,1,0:T(8,128)S(1)} %get-tuple-element.10), kind=kLoop, calls=%fused_computation.49 | loop fusion | flops 2326528 | bytes 262144 | tf_op jit(solution)/shard_map/jit(_where)/select_n | solution.py:56
  3.1 69.8 %shard_map.104 = (f32[16,256,256]{2,1,0:T(8,128)}, f32[4,32,256]{2,1,0:T(8,128)}) custom-call(bf16[16,256,256]{2,1,0:T(8,128)(2,1)} %tiles_hbm.1, s32[2048]{0:T(1024)} %patch_s.1, f32[2048]{0:T(1024)} %weight_s.1, f32[16,10]{1,0:T(8,128)} %coeff_s.1, s32[16,128]{1,0:T(8,128)} %bitcast.6, f32[16,128]{1,0:T(8,128)} %bitcast.7, ...), custom_call_target="tpu_custom_call" | custom-call | tf_op jit(solution)/shard_map/pallas_call | solution.py:542
  73.0 1.6 %copy.13 = f32[4,32,256]{2,1,0:T(8,128)} copy(f32[4,32,256]{2,1,0:T(8,128)} %get-tuple-element.13) | data formatting | bytes 262144
  74.5 4.6 %copy.14 = f32[16,256,256]{2,1,0:T(8,128)} copy(f32[16,256,256]{2,1,0:T(8,128)} %get-tuple-element.14) | data formatting | bytes 8388608
  (1 shorter events, 0.0 us)

commit v2 on v1

v2 whole, which is shorter than its diff:
```python
import functools
import math

import jax
import jax.numpy as jnp
import numpy as np
from jax import lax
from jax.experimental import pallas as pl
from jax.experimental.pallas import tpu as pltpu
from jax.sharding import PartitionSpec as P

MESH = pl.DeviceIdType.MESH
KHALF = 10
SIDE = 256
TILES_DEV = 16
SIGMAS = (1.0, 2.5, 5.0)
FACTORS = ((0, 0), (0, 1), (0, 2), (1, 0), (1, 1), (2, 0))
BASIS_ROWS = (0, 1, 0, 2, 0, 1, 3, 4, 3, 5)
BASIS_COLS = (0, 0, 1, 0, 2, 1, 3, 3, 4, 5)
NF = len(FACTORS)

UNITS = ((0, 3), (3, 6), (6, 8))
GROUPS = 2
TG = TILES_DEV // GROUPS
PG = TG // 2
RB = TG * 8


def wrapped_diff():
    diff = np.arange(128)[None, :] - np.arange(8)[:, None]
    return ((diff + 64) % 128) - 64


def factor_strips():
    diff = wrapped_diff().astype(np.float64)
    reach = np.arange(-KHALF, KHALF + 1).astype(np.float64)
    ahead, back = [], []
    for sigma_index, power in FACTORS:
        sigma = SIGMAS[sigma_index]
        norm = np.sum(np.exp(-reach * reach / (2.0 * sigma * sigma)))
        for out, u in ((ahead, diff), (back, -diff)):
            value = np.exp(-u * u / (2.0 * sigma * sigma)) * (u / sigma) ** power / norm
            out.append(np.where(np.abs(u) <= KHALF, value, 0.0))
    return np.stack(ahead).astype(np.float32), np.stack(back).astype(np.float32)


def sinc(v):
    scaled = math.pi * jnp.where(v == 0.0, 1.0, v)
    return jnp.where(v == 0.0, 1.0, jnp.sin(scaled) / scaled)


def lanczos(offset):
    return jnp.where(jnp.abs(offset) < 3.0, sinc(offset) * sinc(offset / 3.0), 0.0)


def by_portion(p, values):
    return jnp.where(p == 0, values[0], jnp.where(p == 1, values[1], values[2]))


def toeplitz_blocks(strip):
    lane = lax.broadcasted_iota(jnp.int32, (8, 128), 1)
    rows = [strip if b == 0 else pltpu.roll(strip, 8 * b, 1) for b in range(16)]
    low = lane < 64
    zero = jnp.zeros_like(strip)
    left = [jnp.where(low, zero, rows[b]) for b in (0, 1)]
    right = [jnp.where(low, rows[b], zero) for b in (14, 15)]
    for b in (0, 1):
        rows[b] = jnp.where(low, rows[b], zero)
    for b in (14, 15):
        rows[b] = jnp.where(low, zero, rows[b])

    def pack(pair):
        return jnp.concatenate(pair, axis=0).astype(jnp.bfloat16)

    return [pack(rows[2 * i : 2 * i + 2]) for i in range(8)], pack(right), pack(left)


def write_square(strip, ref):
    diag, right, left = toeplitz_blocks(strip)
    for i in range(8):
        ref[16 * i : 16 * i + 16, 0:128] = diag[i]
        ref[128 + 16 * i : 144 + 16 * i, 128:256] = diag[i]
    ref[112:128, 128:256] = right
    ref[128:144, 0:128] = left


def kernel(
    tiles_hbm,
    whole_s,
    part_s,
    patch_s,
    weight_s,
    coeff_s,
    patch_v,
    weight_v,
    ahead,
    back,
    diff_hbm,
    coadd_out,
    tiles,
    warp,
    send1,
    recv1,
    sel,
    asend,
    arecv,
    bsend,
    brecv,
    gath,
    gathf,
    send4,
    recv4,
    csend,
    crecv,
    den,
    strips,
    fmat,
    mband,
    rmat,
    tbuf,
    hbuf,
    rows_s,
    s1,
    r1,
    sa,
    ra,
    sb,
    rb,
    sgb,
    rgb,
    sga,
    rga,
    s4,
    r4,
    sc,
    rc,
    in_sem,
    own1,
    own4,
    out_sem,
):
    visit, sky = lax.axis_index("visit"), lax.axis_index("sky")
    y, c = lax.div(visit, 2), lax.rem(visit, 2)
    z, x = lax.div(sky, 4), lax.rem(sky, 4)

    def dev(y_, c_, z_, x_):
        return (y_ * 2 + c_, z_ * 4 + x_)

    ring_of = (y, z, x)
    first_of, second_of = (x, y, z), (z, x, y)

    def on_ring(p, pos, core):
        return (dev(pos, core, z, x), dev(y, core, pos, x), dev(y, core, z, pos))[p]

    def on_first(p, pos):
        return (dev(y, c, z, pos), dev(pos, c, z, x), dev(y, c, pos, x))[p]

    def on_second(p, pos):
        return (dev(y, c, pos, x), dev(y, c, z, pos), dev(pos, c, z, x))[p]

    def partner(p, k):
        d, core = lax.div(k, 2), lax.rem(c + lax.rem(k, 2), 2)
        return lax.rem(ring_of[p] + d, 4), lax.rem(ring_of[p] + 4 - d, 4), core

    swap = (dev(z, c, y, x), dev(x, c, z, y))
    moved = (y != z, y != x)

    def fetch(g):
        return pltpu.make_async_copy(
            tiles_hbm.at[pl.ds(g * TG, TG)], tiles.at[pl.ds(g * TG, TG)], in_sem.at[g]
        )

    for g in range(GROUPS):
        fetch(g).start()

    barrier = pltpu.get_barrier_semaphore()
    pl.semaphore_signal(barrier, inc=1, device_id=dev(y, 1 - c, z, x), device_id_type=MESH)
    for p in range(3):

        @pl.loop(2, 8)
        def _(k, p=p):
            pos, unused, core = partner(p, k)
            pl.semaphore_signal(barrier, inc=1, device_id=on_ring(p, pos, core), device_id_type=MESH)

    for i in range(2):

        @pl.when(moved[i])
        def _(i=i):
            pl.semaphore_signal(barrier, inc=1, device_id=swap[i], device_id_type=MESH)

    lane = lax.broadcasted_iota(jnp.int32, (8, 128), 1)
    down = lax.broadcasted_iota(jnp.int32, (8, 128), 0)
    reach = jnp.where(lane < 64, lane, lane - 128).astype(jnp.float32)
    reach = jnp.where((down & 1) == 0, reach, -reach)

    @pl.loop(0, 4)
    def _(i):
        shift = jnp.zeros((8, 128), jnp.float32)
        for r in range(8):
            t = i * 4 + r // 2
            value = whole_s[r % 2, t].astype(jnp.float32) + part_s[r % 2, t]
            shift = jnp.where(down == r, value, shift)
        taps = lanczos(reach - shift)
        for r in range(8):
            row = jnp.broadcast_to(taps[r : r + 1], (8, 128))
            strips[i * 8 + r] = pltpu.roll(row, 0, 1, stride=1, stride_axis=0)

    @pl.loop(0, 4)
    def _(j):
        rmat[j] = jnp.zeros((SIDE, SIDE), jnp.bfloat16)

    def own_first(p, g):
        lo, hi = UNITS[p]
        return pltpu.make_async_copy(
            send1.at[g, ring_of[p] * 2 + c, pl.ds(lo, hi - lo)],
            recv1.at[g, 0, pl.ds(lo, hi - lo)],
            own1.at[p, g],
        )

    def first(p, g, k):
        lo, hi = UNITS[p]
        pos, unused, core = partner(p, k)
        return pltpu.make_async_remote_copy(
            src_ref=send1.at[g, pos * 2 + core, pl.ds(lo, hi - lo)],
            dst_ref=recv1.at[g, k, pl.ds(lo, hi - lo)],
            send_sem=s1.at[p, g, k - 1],
            recv_sem=r1.at[p, g, k - 1],
            device_id=on_ring(p, pos, core),
            device_id_type=MESH,
        )

    @pl.loop(0, GROUPS)
    def _(g):
        fetch(g).wait()

        @pl.loop(0, PG)
        def _(pair):
            scaled = []
            for half in range(2):
                t = g * TG + pair * 2 + half
                write_square(strips[2 * t], rmat.at[2 * half])
                write_square(strips[2 * t + 1], rmat.at[2 * half + 1])
                rowpass = jnp.dot(
                    tiles[t], rmat[2 * half + 1], preferred_element_type=jnp.float32
                ).astype(jnp.bfloat16)
                value = jnp.dot(rmat[2 * half], rowpass, preferred_element_type=jnp.float32)
                warp[t] = value
                scaled.append((weight_s[(visit * 16 + sky) * TILES_DEV + t] * value).reshape(32, 8, SIDE))
            both = jnp.concatenate(scaled, axis=1).astype(jnp.bfloat16)
            rows = pl.ds(pl.multiple_of(pair * 16, 16), 16)
            for q in range(8):
                for u in range(8):
                    send1[g, q, u, rows, :] = both[4 * q + u // 2, :, 128 * (u % 2) : 128 * (u % 2) + 128]

        @pl.when(g == 0)
        def _():
            pl.semaphore_wait(barrier, 19 + moved[0].astype(jnp.int32) + moved[1].astype(jnp.int32))

        @pl.loop(1, 8)
        def _(k):
            for p in range(3):
                first(p, g, k).start()

        for p in range(3):
            own_first(p, g).start()

    for p in range(3):

        @pl.loop(0, 8)
        def _(k, p=p):
            unused, pos, core = partner(p, k)
            v, s = on_ring(p, pos, core)
            base = (v * 16 + s) * TILES_DEV
            for g in range(GROUPS):
                for tt in range(TG):
                    patch = patch_s[base + g * TG + tt]
                    if p == 0:
                        patch = ((patch >> 2) & 3) * 16 + (patch >> 4) * 4 + (patch & 3)
                    rows_s[p, g * 8 * TG + k * TG + tt] = patch

    high = lax.broadcasted_iota(jnp.int32, (512, 128), 0)

    @pl.loop(0, 24)
    def _(n):
        p, m = lax.div(n, 8), lax.rem(n, 8)
        key = jnp.zeros((8, 128), jnp.int32)
        for tt in range(16):
            key = jnp.where((lane >> 3) == tt, rows_s[p, m * 16 + tt], key)
        key = key * 8 + (lane & 7)
        wide = jnp.broadcast_to(key[0:1], (512, 128))
        sel[p, :, pl.ds(pl.multiple_of(m * 128, 128), 128)] = jnp.where(wide == high, 1.0, 0.0).astype(
            jnp.bfloat16
        )

    @pl.loop(0, 12)
    def _(n):
        p, k = lax.div(n, 4), lax.rem(n, 4)
        owner = by_portion(p, (z * 4 + x, y * 4 + x, z * 4 + y))
        hit = jnp.where(patch_v[...] == owner * 4 + k, weight_v[...], 0.0)
        weight = jnp.sum(jnp.sum(hit, axis=0, keepdims=True), axis=1, keepdims=True)
        den[p, pl.ds(pl.multiple_of(k * 8, 8), 8)] = jnp.broadcast_to(1.0 + weight, (8, 128))

    @pl.loop(0, NF)
    def _(j):
        fmat[j] = jnp.zeros((SIDE, SIDE), jnp.bfloat16)
        write_square(ahead[j], fmat.at[j])

    @pl.loop(0, TILES_DEV)
    def _(t):
        for j in range(NF):
            strip = None
            for k in range(len(BASIS_COLS)):
                if BASIS_COLS[k] == j:
                    term = coeff_s[t, k] * back[BASIS_ROWS[k]]
                    strip = term if strip is None else strip + term
            diag, right, left = toeplitz_blocks(strip)
            cols = slice(128 * j, 128 * j + 128)
            mband[t, 0:16, cols] = right
            for i in range(8):
                mband[t, 16 + 16 * i : 32 + 16 * i, cols] = diag[i]
            mband[t, 144:160, cols] = left

    def second(p, d):
        lo, hi = UNITS[p]
        pos = lax.rem(first_of[p] + d, 4)
        return pltpu.make_async_remote_copy(
            src_ref=asend.at[pos, pl.ds(lo, hi - lo)],
            dst_ref=arecv.at[d - 1, pl.ds(lo, hi - lo)],
            send_sem=sa.at[p, d - 1],
            recv_sem=ra.at[p, d - 1],
            device_id=on_first(p, pos),
            device_id_type=MESH,
        )

    def third(p, d):
        lo, hi = UNITS[p]
        pos = lax.rem(second_of[p] + d, 4)
        return pltpu.make_async_remote_copy(
            src_ref=bsend.at[pos, pl.ds(lo, hi - lo)],
            dst_ref=brecv.at[d - 1, pl.ds(lo, hi - lo)],
            send_sem=sb.at[p, d - 1],
            recv_sem=rb.at[p, d - 1],
            device_id=on_second(p, pos),
            device_id_type=MESH,
        )

    def fourth(p, d):
        lo, hi = UNITS[p]
        mine = gath.at[first_of[p], second_of[p], pl.ds(lo, hi - lo)]
        return pltpu.make_async_remote_copy(
            src_ref=mine,
            dst_ref=mine,
            send_sem=sgb.at[p, d - 1],
            recv_sem=rgb.at[p, d - 1],
            device_id=on_second(p, lax.rem(second_of[p] + d, 4)),
            device_id_type=MESH,
        )

    def fifth(p, d):
        lo, hi = UNITS[p]
        mine = gath.at[first_of[p], :, pl.ds(lo, hi - lo)]
        return pltpu.make_async_remote_copy(
            src_ref=mine,
            dst_ref=mine,
            send_sem=sga.at[p, d - 1],
            recv_sem=rga.at[p, d - 1],
            device_id=on_first(p, lax.rem(first_of[p] + d, 4)),
            device_id_type=MESH,
        )

    def each_unit(before, body, after):
        @pl.loop(0, 8)
        def _(u):
            for p in range(3):

                @pl.when(u == UNITS[p][0])
                def _(p=p):
                    before(p)

            body(u, lax.div(u, 3))
            for p in range(3):

                @pl.when(u == UNITS[p][1] - 1)
                def _(p=p):
                    after(p)

    def all_three(act):
        @pl.loop(1, 4)
        def _(d):
            act(d)

    def arrived(p):
        @pl.loop(0, GROUPS)
        def _(g):
            own_first(p, g).wait()

            @pl.loop(1, 8)
            def _(k):
                first(p, g, k).wait_recv()

    def add_tiles(u, p):
        total = jnp.dot(sel[p], recv1[:, :, u].reshape(1024, 128), preferred_element_type=jnp.float32)
        asend[:, u] = total.astype(jnp.bfloat16).reshape(4, 128, 128)

    each_unit(arrived, add_tiles, lambda p: all_three(lambda d: second(p, d).start()))

    def add_first(u, p):
        total = asend[by_portion(p, first_of), u].astype(jnp.float32)
        for d in range(3):
            total = total + arecv[d, u].astype(jnp.float32)
        total = total.astype(jnp.bfloat16)
        for b in range(4):
            bsend[b, u] = total[32 * b : 32 * b + 32]

    each_unit(
        lambda p: all_three(lambda d: second(p, d).wait_recv()),
        add_first,
        lambda p: all_three(lambda d: third(p, d).start()),
    )

    def add_second(u, p):
        mine = by_portion(p, second_of)
        total = bsend[mine, u].astype(jnp.float32)
        for d in range(3):
            total = total + brecv[d, u].astype(jnp.float32)
        coadd = total / den[p]
        csend[u] = coadd
        gath[by_portion(p, first_of), mine, u] = coadd.astype(jnp.bfloat16)

    each_unit(
        lambda p: all_three(lambda d: third(p, d).wait_recv()),
        add_second,
        lambda p: all_three(lambda d: fourth(p, d).start()),
    )

    def to_owner(i):
        lo, hi = UNITS[i + 1]
        return pltpu.make_async_remote_copy(
            src_ref=csend.at[pl.ds(lo, hi - lo)],
            dst_ref=crecv.at[pl.ds(lo, hi - lo)],
            send_sem=sc.at[i],
            recv_sem=rc.at[i],
            device_id=swap[i],
            device_id_type=MESH,
        )

    for i in range(2):

        @pl.when(moved[i])
        def _(i=i):
            to_owner(i).start()

    for p in range(3):
        all_three(lambda d, p=p: fourth(p, d).wait_recv())
        all_three(lambda d, p=p: fifth(p, d).start())

    def own_last(p, g):
        lo, hi = UNITS[p]
        return pltpu.make_async_copy(
            send4.at[g, 0, pl.ds(lo, hi - lo)],
            recv4.at[g, ring_of[p] * 2 + c, pl.ds(lo, hi - lo)],
            own4.at[p, g],
        )

    def last(p, g, k):
        lo, hi = UNITS[p]
        unused, pos, core = partner(p, k)
        return pltpu.make_async_remote_copy(
            src_ref=send4.at[g, k, pl.ds(lo, hi - lo)],
            dst_ref=recv4.at[g, ring_of[p] * 2 + c, pl.ds(lo, hi - lo)],
            send_sem=s4.at[p, g, k - 1],
            recv_sem=r4.at[p, g, k - 1],
            device_id=on_ring(p, pos, core),
            device_id_type=MESH,
        )

    @pl.loop(0, GROUPS)
    def _(g):
        for p in range(3):
            lo, hi = UNITS[p]

            @pl.when(g == 0)
            def _(p=p, lo=lo, hi=hi):
                all_three(lambda d: fifth(p, d).wait_recv())

                @pl.loop(lo, hi)
                def _(u):
                    gathf[u] = gath[:, :, u].reshape(64, 8, 128).astype(jnp.float32)

            @pl.loop(0, 8)
            def _(k, p=p, lo=lo, hi=hi):
                for pair in range(PG):
                    at = g * 8 * TG + k * TG + 2 * pair
                    one, two = rows_s[p, at], rows_s[p, at + 1]
                    for u in range(lo, hi):
                        send4[g, k, u, 16 * pair : 16 * pair + 16, :] = jnp.concatenate(
                            [gathf[u, one], gathf[u, two]], axis=0
                        ).astype(jnp.bfloat16)

            @pl.loop(1, 8)
            def _(k, p=p):
                last(p, g, k).start()

            own_last(p, g).start()

    def leave(g, pair):
        t = g * TG + pair * 2
        return pltpu.make_async_copy(
            warp.at[pl.ds(t, 2)], diff_hbm.at[pl.ds(t, 2)], out_sem.at[g, pair]
        )

    @pl.loop(0, GROUPS)
    def _(g):
        for p in range(3):
            own_last(p, g).wait()

            @pl.loop(1, 8)
            def _(k, p=p):
                last(p, g, k).wait_recv()

        @pl.loop(0, PG)
        def _(pair):
            rows = pl.ds(pl.multiple_of(pair * 16, 16), 16)
            for q in range(8):
                for i in range(2):
                    for b in range(2):
                        upper = recv4[g, q, 4 * i + b, rows, :].astype(jnp.float32)
                        lower = recv4[g, q, 4 * i + 2 + b, rows, :].astype(jnp.float32)
                        at = 32 * q + 16 * i
                        cols = slice(128 * b, 128 * b + 128)
                        tbuf[at : at + 16, cols] = jnp.concatenate(
                            [upper[0:8], lower[0:8]], axis=0
                        ).astype(jnp.bfloat16)
                        tbuf[SIDE + at : SIDE + at + 16, cols] = jnp.concatenate(
                            [upper[8:16], lower[8:16]], axis=0
                        ).astype(jnp.bfloat16)
            for j in range(NF):
                filtered = jnp.dot(
                    tbuf[...], fmat[j], preferred_element_type=jnp.float32
                ).astype(jnp.bfloat16)
                for i in range(4):
                    hbuf[i, 128 * j : 128 * j + 128, :] = filtered[128 * i : 128 * i + 128]
            for half in range(2):
                t = g * TG + pair * 2 + half
                top = jnp.dot(
                    mband[t, 16:160, :], hbuf[2 * half], preferred_element_type=jnp.float32
                )
                low = jnp.dot(
                    mband[t, 0:144, :], hbuf[2 * half + 1], preferred_element_type=jnp.float32
                )
                warp[t, 0:112] = warp[t, 0:112] - top[0:112]
                warp[t, 112:144] = warp[t, 112:144] - (top[112:144] + low[0:32])
                warp[t, 144:256] = warp[t, 144:256] - low[32:144]
            leave(g, pair).start()

    for i in range(2):
        lo, hi = UNITS[i + 1]

        @pl.when(moved[i])
        def _(i=i):
            to_owner(i).wait()

        @pl.when(jnp.logical_not(moved[i]))
        def _(lo=lo, hi=hi):
            crecv[lo:hi] = csend[lo:hi]

    for u in range(8):
        held = csend if u < UNITS[0][1] else crecv
        for k in range(4):
            coadd_out[k, 8 * (u // 2) : 8 * (u // 2) + 8, 128 * (u % 2) : 128 * (u % 2) + 128] = held[
                u, 8 * k : 8 * k + 8
            ]

    for p in range(3):

        @pl.loop(0, GROUPS)
        def _(g, p=p):
            @pl.loop(1, 8)
            def _(k):
                first(p, g, k).wait_send()
                last(p, g, k).wait_send()

        @pl.loop(1, 4)
        def _(d, p=p):
            second(p, d).wait_send()
            third(p, d).wait_send()
            fourth(p, d).wait_send()
            fifth(p, d).wait_send()

    @pl.loop(0, GROUPS)
    def _(g):
        @pl.loop(0, PG)
        def _(pair):
            leave(g, pair).wait()


def shards(tiles, shift_int, shift_frac, tile_weight, tile_patch, al_coeff):
    ahead, back = factor_strips()
    vmem = pl.BlockSpec(memory_space=pltpu.VMEM)
    smem = pl.BlockSpec(memory_space=pltpu.SMEM)
    hbm = pl.BlockSpec(memory_space=pl.ANY)
    bf16, f32 = jnp.bfloat16, jnp.float32
    dma = pltpu.SemaphoreType.DMA
    block = (GROUPS, 8, 8, RB, 128)
    difference, coadd = pl.pallas_call(
        kernel,
        out_shape=(
            jax.ShapeDtypeStruct((TILES_DEV, SIDE, SIDE), f32),
            jax.ShapeDtypeStruct((4, 32, SIDE), f32),
        ),
        in_specs=[hbm, smem, smem, smem, smem, smem, vmem, vmem, vmem, vmem],
        out_specs=(hbm, vmem),
        scratch_shapes=[
            pltpu.VMEM((TILES_DEV, SIDE, SIDE), bf16),
            pltpu.VMEM((TILES_DEV, SIDE, SIDE), f32),
            pltpu.VMEM(block, bf16),
            pltpu.VMEM(block, bf16),
            pltpu.VMEM((3, 512, 1024), bf16),
            pltpu.VMEM((4, 8, 128, 128), bf16),
            pltpu.VMEM((3, 8, 128, 128), bf16),
            pltpu.VMEM((4, 8, 32, 128), bf16),
            pltpu.VMEM((3, 8, 32, 128), bf16),
            pltpu.VMEM((4, 4, 8, 32, 128), bf16),
            pltpu.VMEM((8, 64, 8, 128), f32),
            pltpu.VMEM(block, bf16),
            pltpu.VMEM(block, bf16),
            pltpu.VMEM((8, 32, 128), f32),
            pltpu.VMEM((8, 32, 128), f32),
            pltpu.VMEM((3, 32, 128), f32),
            pltpu.VMEM((2 * TILES_DEV, 8, 128), f32),
            pltpu.VMEM((NF, SIDE, SIDE), bf16),
            pltpu.VMEM((TILES_DEV, 160, 128 * NF), bf16),
            pltpu.VMEM((4, SIDE, SIDE), bf16),
            pltpu.VMEM((2 * SIDE, SIDE), bf16),
            pltpu.VMEM((4, 128 * NF, SIDE), bf16),
            pltpu.SMEM((3, 128), jnp.int32),
            dma((3, GROUPS, 7)),
            dma((3, GROUPS, 7)),
            dma((3, 3)),
            dma((3, 3)),
            dma((3, 3)),
            dma((3, 3)),
            dma((3, 3)),
            dma((3, 3)),
            dma((3, 3)),
            dma((3, 3)),
            dma((3, GROUPS, 7)),
            dma((3, GROUPS, 7)),
            dma((2,)),
            dma((2,)),
            dma((GROUPS,)),
            dma((3, GROUPS)),
            dma((3, GROUPS)),
            dma((GROUPS, PG)),
        ],
        compiler_params=pltpu.CompilerParams(
            collective_id=0, has_side_effects=True, vmem_limit_bytes=56 << 20
        ),
    )(
        tiles,
        shift_int.T,
        shift_frac.T,
        tile_patch,
        tile_weight,
        al_coeff,
        tile_patch.reshape(16, 128),
        tile_weight.reshape(16, 128),
        jnp.asarray(ahead),
        jnp.asarray(back),
    )
    return coadd, difference


def solution(mesh):
    return jax.shard_map(
        shards,
        mesh=mesh,
        in_specs=(
            P(("visit", "sky"), None, None),
            P(("visit", "sky"), None),
            P(("visit", "sky"), None),
            P(),
            P(),
            P(("visit", "sky"), None),
        ),
        out_specs=(P("sky", "visit", None), P(("visit", "sky"), None, None)),
        check_vma=False,
    )
```

time: 79.4 us -> 69.1 us (0.87)
  Pallas kernels: 69.8 us -> 62 us
  other arithmetic: 2.47 us -> 0 us
    pallas_call x1, Pallas kernels: 69.8 us -> 62 us  [shards(): pl.pallas_call(kernel, out_shape=(jax.ShapeDtypeStruct((TILES_DEV, SIDE,...]
    select_n x1 -> x0, other arithmetic: 0.97 us -> none  [lanczos_strips(): jnp.where(jnp.abs(offset) < 3.0, jnp.sinc(offset) * jnp.sinc(offset / 3.0...]
    sub x1 -> x0, other arithmetic: 0.8 us -> none  [lanczos_strips(): -diff[None] - shift[:, 1, None, None]]
where the time goes in v2:
time: 69.1 us; the launch traced here: 68.8 us
  Pallas kernels  62 us (90%)
  local copies, waits for them, and re-layouts  6.16 us (9%)
    pallas_call x1, Pallas kernels, shards(): pl.pallas_call(kernel, out_shape=(jax.ShapeDtypeStruct((TILES_DEV, SIDE,...  62 us
    unnamed x2, local copies, waits for them, and re-layouts  6.16 us

profile of v2, /device:TPU:1, one launch (start us, length us, event | category | flops | bytes accessed | tf_op | source)
XLA Modules:
  0.0 68.8 jit_solution(13814690176889785505)
XLA Ops:
  0.6 62.0 %shard_map.95 = (f32[16,256,256]{2,1,0:T(8,128)}, f32[4,32,256]{2,1,0:T(8,128)}) custom-call(bf16[16,256,256]{2,1,0:T(8,128)(2,1)} %tiles_hbm.1, s32[2,16]{1,0:T(2,128)} %bitcast.6, f32[2,16]{1,0:T(2,128)} %bitcast.7, s32[2048]{0:T(1024)} %patch_s.1, f32[2048]{0:T(1024)} %weight_s.1, f32[16,10]{1,0:T(8,128)} %coeff_s.1, s32[16,128]{1,0:T(8,128)} %bitcast.4, ...), custom_call_target="tpu_custom_call" | custom-call | tf_op jit(solution)/shard_map/pallas_call | solution.py:605
  62.7 1.6 %copy.12 = f32[4,32,256]{2,1,0:T(8,128)} copy(f32[4,32,256]{2,1,0:T(8,128)} %get-tuple-element.8) | data formatting | bytes 262144
  64.2 4.6 %copy.13 = f32[16,256,256]{2,1,0:T(8,128)} copy(f32[16,256,256]{2,1,0:T(8,128)} %get-tuple-element.9) | data formatting | bytes 8388608

commit v3 on v2

v3 whole, which is shorter than its diff:
```python
import functools
import math

import jax
import jax.numpy as jnp
import numpy as np
from jax import lax
from jax.experimental import pallas as pl
from jax.experimental.pallas import tpu as pltpu
from jax.sharding import PartitionSpec as P

MESH = pl.DeviceIdType.MESH
KHALF = 10
SIDE = 256
TILES_DEV = 16
SIGMAS = (1.0, 2.5, 5.0)
FACTORS = ((0, 0), (0, 1), (0, 2), (1, 0), (1, 1), (2, 0))
BASIS_ROWS = (0, 1, 0, 2, 0, 1, 3, 4, 3, 5)
BASIS_COLS = (0, 0, 1, 0, 2, 1, 3, 3, 4, 5)
NF = len(FACTORS)

SEGMENTS = ((0, 0, 2), (1, 2, 3), (2, 3, 4), (0, 4, 5), (1, 5, 7), (2, 7, 8))
FIRST_WAVE, SECOND_WAVE = (0, 1, 2), (3, 4, 5)
GROUPS = 2
TG = TILES_DEV // GROUPS
PG = TG // 2
RB = TG * 8


def wrapped_diff():
    diff = np.arange(128)[None, :] - np.arange(8)[:, None]
    return ((diff + 64) % 128) - 64


def factor_strips():
    diff = wrapped_diff().astype(np.float64)
    reach = np.arange(-KHALF, KHALF + 1).astype(np.float64)
    ahead, back = [], []
    for sigma_index, power in FACTORS:
        sigma = SIGMAS[sigma_index]
        norm = np.sum(np.exp(-reach * reach / (2.0 * sigma * sigma)))
        for out, u in ((ahead, diff), (back, -diff)):
            value = np.exp(-u * u / (2.0 * sigma * sigma)) * (u / sigma) ** power / norm
            out.append(np.where(np.abs(u) <= KHALF, value, 0.0))
    return np.stack(ahead).astype(np.float32), np.stack(back).astype(np.float32)


def sinc(v):
    scaled = math.pi * jnp.where(v == 0.0, 1.0, v)
    return jnp.where(v == 0.0, 1.0, jnp.sin(scaled) / scaled)


def lanczos(offset):
    return jnp.where(jnp.abs(offset) < 3.0, sinc(offset) * sinc(offset / 3.0), 0.0)


def by_portion(p, values):
    return jnp.where(p == 0, values[0], jnp.where(p == 1, values[1], values[2]))


def portion_of(u):
    return jnp.where((u == 3) | (u == 7), 2, jnp.where((u == 2) | (u == 5) | (u == 6), 1, 0))


def toeplitz_blocks(strip):
    lane = lax.broadcasted_iota(jnp.int32, (8, 128), 1)
    rows = [strip if b == 0 else pltpu.roll(strip, 8 * b, 1) for b in range(16)]
    low = lane < 64
    zero = jnp.zeros_like(strip)
    left = [jnp.where(low, zero, rows[b]) for b in (0, 1)]
    right = [jnp.where(low, rows[b], zero) for b in (14, 15)]
    for b in (0, 1):
        rows[b] = jnp.where(low, rows[b], zero)
    for b in (14, 15):
        rows[b] = jnp.where(low, zero, rows[b])

    def pack(pair):
        return jnp.concatenate(pair, axis=0).astype(jnp.bfloat16)

    return [pack(rows[2 * i : 2 * i + 2]) for i in range(8)], pack(right), pack(left)


def write_square(strip, ref):
    diag, right, left = toeplitz_blocks(strip)
    for i in range(8):
        ref[16 * i : 16 * i + 16, 0:128] = diag[i]
        ref[128 + 16 * i : 144 + 16 * i, 128:256] = diag[i]
    ref[112:128, 128:256] = right
    ref[128:144, 0:128] = left


def exchange(
    tiles_hbm,
    whole_s,
    part_s,
    coeff_s,
    patch_1d,
    weight_1d,
    patch_2d,
    weight_2d,
    back_hbm,
    warp_hbm,
    mband_hbm,
    recv4,
    coadd_hbm,
    tiles,
    warp,
    send1,
    recv1,
    sel,
    asend,
    arecv,
    bsend,
    brecv,
    gath,
    gathf,
    send4,
    cfull,
    crecv,
    hits,
    den,
    strips,
    mband,
    rmat,
    patch_v,
    weight_v,
    back,
    rows_s,
    patch_s,
    weight_s,
    s1,
    r1,
    s1b,
    r1b,
    sa,
    ra,
    sb,
    rb,
    sga,
    rga,
    s4,
    r4,
    sc,
    rc,
    in_sem,
    small_sem,
    own1,
    own4,
    out_sem,
):
    visit, sky = lax.axis_index("visit"), lax.axis_index("sky")
    y, c = lax.div(visit, 2), lax.rem(visit, 2)
    z, x = lax.div(sky, 4), lax.rem(sky, 4)

    def dev(y_, c_, z_, x_):
        return (y_ * 2 + c_, z_ * 4 + x_)

    ring_of = (y, z, x)
    first_of, second_of = (x, y, z), (z, x, y)

    def on_ring(p, pos, core):
        return (dev(pos, core, z, x), dev(y, core, pos, x), dev(y, core, z, pos))[p]

    def on_first(p, pos):
        return (dev(y, c, z, pos), dev(pos, c, z, x), dev(y, c, pos, x))[p]

    def on_second(p, pos):
        return (dev(y, c, pos, x), dev(y, c, z, pos), dev(pos, c, z, x))[p]

    def partner(p, k):
        d, core = lax.div(k, 2), lax.rem(c + lax.rem(k, 2), 2)
        return lax.rem(ring_of[p] + d, 4), lax.rem(ring_of[p] + 4 - d, 4), core

    swap = (dev(z, c, y, x), dev(x, c, z, y))
    moved = (y != z, y != x)

    def fetch(g):
        return pltpu.make_async_copy(
            tiles_hbm.at[pl.ds(g * TG, TG)], tiles.at[pl.ds(g * TG, TG)], in_sem.at[g]
        )

    small = [
        pltpu.make_async_copy(here, there, small_sem.at[i])
        for i, (here, there) in enumerate(
            (
                (weight_1d, weight_s),
                (patch_1d, patch_s),
                (patch_2d, patch_v),
                (weight_2d, weight_v),
                (back_hbm, back),
            )
        )
    ]

    barrier = pltpu.get_barrier_semaphore()
    pl.semaphore_signal(barrier, inc=1, device_id=dev(y, 1 - c, z, x), device_id_type=MESH)
    for p in range(3):

        @pl.loop(2, 8)
        def _(k, p=p):
            pos, unused, core = partner(p, k)
            pl.semaphore_signal(barrier, inc=1, device_id=on_ring(p, pos, core), device_id_type=MESH)

    for i in range(2):

        @pl.when(moved[i])
        def _(i=i):
            pl.semaphore_signal(barrier, inc=1, device_id=swap[i], device_id_type=MESH)

    for g in range(GROUPS):
        fetch(g).start()
    for copy in small:
        copy.start()

    lane = lax.broadcasted_iota(jnp.int32, (8, 128), 1)
    down = lax.broadcasted_iota(jnp.int32, (8, 128), 0)
    reach = jnp.where(lane < 64, lane, lane - 128).astype(jnp.float32)
    reach = jnp.where((down & 1) == 0, reach, -reach)

    @pl.loop(0, 4)
    def _(i):
        shift = jnp.zeros((8, 128), jnp.float32)
        for r in range(8):
            t = i * 4 + r // 2
            value = whole_s[r % 2, t].astype(jnp.float32) + part_s[r % 2, t]
            shift = jnp.where(down == r, value, shift)
        taps = lanczos(reach - shift)
        for r in range(8):
            row = jnp.broadcast_to(taps[r : r + 1], (8, 128))
            strips[i * 8 + r] = pltpu.roll(row, 0, 1, stride=1, stride_axis=0)

    @pl.loop(0, 4)
    def _(j):
        rmat[j] = jnp.zeros((SIDE, SIDE), jnp.bfloat16)

    def at_group(ref, g, slot, lo, hi):
        units = pl.ds(lo, hi - lo)
        return ref.at[:, slot, units] if g is None else ref.at[g, slot, units]

    def own_first(n, g):
        p, lo, hi = SEGMENTS[n]
        return pltpu.make_async_copy(
            at_group(send1, g, ring_of[p] * 2 + c, lo, hi),
            at_group(recv1, g, 0, lo, hi),
            own1.at[n, 0 if g is None else g],
        )

    def first(n, g, k):
        p, lo, hi = SEGMENTS[n]
        pos, unused, core = partner(p, k)
        return pltpu.make_async_remote_copy(
            src_ref=at_group(send1, g, pos * 2 + core, lo, hi),
            dst_ref=at_group(recv1, g, k, lo, hi),
            send_sem=s1b.at[p, k - 1] if g is None else s1.at[p, g, k - 1],
            recv_sem=r1b.at[p, k - 1] if g is None else r1.at[p, g, k - 1],
            device_id=on_ring(p, pos, core),
            device_id_type=MESH,
        )

    small[0].wait()

    @pl.loop(0, GROUPS)
    def _(g):
        fetch(g).wait()

        @pl.loop(0, PG)
        def _(pair):
            scaled = []
            for half in range(2):
                t = g * TG + pair * 2 + half
                write_square(strips[2 * t], rmat.at[2 * half])
                write_square(strips[2 * t + 1], rmat.at[2 * half + 1])
                rowpass = jnp.dot(
                    tiles[t], rmat[2 * half + 1], preferred_element_type=jnp.float32
                ).astype(jnp.bfloat16)
                value = jnp.dot(rmat[2 * half], rowpass, preferred_element_type=jnp.float32)
                warp[t] = value
                scaled.append((weight_s[(visit * 16 + sky) * TILES_DEV + t] * value).reshape(32, 8, SIDE))
            both = jnp.concatenate(scaled, axis=1).astype(jnp.bfloat16)
            rows = pl.ds(pl.multiple_of(pair * 16, 16), 16)
            for q in range(8):
                for u in range(8):
                    send1[g, q, u, rows, :] = both[4 * q + u // 2, :, 128 * (u % 2) : 128 * (u % 2) + 128]

        @pl.when(g == 0)
        def _():
            pl.semaphore_wait(barrier, 19 + moved[0].astype(jnp.int32) + moved[1].astype(jnp.int32))

        @pl.loop(1, 8)
        def _(k):
            for n in FIRST_WAVE:
                first(n, g, k).start()

        for n in FIRST_WAVE:
            own_first(n, g).start()

    @pl.loop(1, 8)
    def _(k):
        for n in SECOND_WAVE:
            first(n, None, k).start()

    for n in SECOND_WAVE:
        own_first(n, None).start()

    keep_warp = pltpu.make_async_copy(warp, warp_hbm, out_sem.at[0])
    keep_warp.start()
    for copy in small[1:]:
        copy.wait()

    for p in range(3):

        @pl.loop(0, 8)
        def _(k, p=p):
            unused, pos, core = partner(p, k)
            v, s = on_ring(p, pos, core)
            base = (v * 16 + s) * TILES_DEV
            for g in range(GROUPS):
                for tt in range(TG):
                    patch = patch_s[base + g * TG + tt]
                    if p == 0:
                        patch = ((patch >> 2) & 3) * 16 + (patch >> 4) * 4 + (patch & 3)
                    rows_s[p, g * 8 * TG + k * TG + tt] = patch

    high = lax.broadcasted_iota(jnp.int32, (512, 128), 0)

    @pl.loop(0, 24)
    def _(n):
        p, m = lax.div(n, 8), lax.rem(n, 8)
        key = jnp.zeros((8, 128), jnp.int32)
        for tt in range(16):
            key = jnp.where((lane >> 3) == tt, rows_s[p, m * 16 + tt], key)
        key = key * 8 + (lane & 7)
        wide = jnp.broadcast_to(key[0:1], (512, 128))
        sel[p, :, pl.ds(pl.multiple_of(m * 128, 128), 128)] = jnp.where(wide == high, 1.0, 0.0).astype(
            jnp.bfloat16
        )

    @pl.loop(0, 48)
    def _(n):
        p, second, k = lax.div(n, 16), lax.rem(lax.div(n, 4), 4), lax.rem(n, 4)
        owner = by_portion(p, (second * 4 + x, y * 4 + second, z * 4 + second))
        hit = jnp.where(patch_v[...] == owner * 4 + k, weight_v[...], 0.0)
        hits[n] = hit[0:8] + hit[8:16]

    weights = 1.0 + jnp.sum(jnp.sum(hits[...], axis=1), axis=1, keepdims=True)
    for n in range(48):
        den[n // 16, 8 * (n % 16) : 8 * (n % 16) + 8] = jnp.broadcast_to(weights[n : n + 1], (8, 128))

    @pl.loop(0, TILES_DEV)
    def _(t):
        for j in range(NF):
            strip = None
            for k in range(len(BASIS_COLS)):
                if BASIS_COLS[k] == j:
                    term = coeff_s[t, k] * back[BASIS_ROWS[k]]
                    strip = term if strip is None else strip + term
            diag, right, left = toeplitz_blocks(strip)
            cols = slice(128 * j, 128 * j + 128)
            mband[t, 0:16, cols] = right
            for i in range(8):
                mband[t, 16 + 16 * i : 32 + 16 * i, cols] = diag[i]
            mband[t, 144:160, cols] = left

    keep_mband = pltpu.make_async_copy(mband, mband_hbm, out_sem.at[1])
    keep_mband.start()

    def second(n, d):
        p, lo, hi = SEGMENTS[n]
        pos = lax.rem(first_of[p] + d, 4)
        return pltpu.make_async_remote_copy(
            src_ref=asend.at[pos, pl.ds(lo, hi - lo)],
            dst_ref=arecv.at[d - 1, pl.ds(lo, hi - lo)],
            send_sem=sa.at[n, d - 1],
            recv_sem=ra.at[n, d - 1],
            device_id=on_first(p, pos),
            device_id_type=MESH,
        )

    def third(n, d):
        p, lo, hi = SEGMENTS[n]
        return pltpu.make_async_remote_copy(
            src_ref=bsend.at[pl.ds(lo, hi - lo)],
            dst_ref=brecv.at[d - 1, pl.ds(lo, hi - lo)],
            send_sem=sb.at[n, d - 1],
            recv_sem=rb.at[n, d - 1],
            device_id=on_second(p, lax.rem(second_of[p] + d, 4)),
            device_id_type=MESH,
        )

    def fourth(n, d):
        p, lo, hi = SEGMENTS[n]
        mine = gath.at[first_of[p], pl.ds(lo, hi - lo)]
        return pltpu.make_async_remote_copy(
            src_ref=mine,
            dst_ref=mine,
            send_sem=sga.at[n, d - 1],
            recv_sem=rga.at[n, d - 1],
            device_id=on_first(p, lax.rem(first_of[p] + d, 4)),
            device_id_type=MESH,
        )

    def each_unit(before, body, after):
        @pl.loop(0, 8)
        def _(u):
            for n, (unused, lo, hi) in enumerate(SEGMENTS):

                @pl.when(u == lo)
                def _(n=n):
                    before(n)

            body(u, portion_of(u))
            for n, (unused, lo, hi) in enumerate(SEGMENTS):

                @pl.when(u == hi - 1)
                def _(n=n):
                    after(n)

    def all_three(act):
        @pl.loop(1, 4)
        def _(d):
            act(d)

    def arrived(n):
        if n in FIRST_WAVE:

            @pl.loop(0, GROUPS)
            def _(g):
                own_first(n, g).wait()

                @pl.loop(1, 8)
                def _(k):
                    first(n, g, k).wait_recv()

        else:
            own_first(n, None).wait()

            @pl.loop(1, 8)
            def _(k):
                first(n, None, k).wait_recv()

    def add_tiles(u, p):
        total = jnp.dot(sel[p], recv1[:, :, u].reshape(1024, 128), preferred_element_type=jnp.float32)
        asend[:, u] = total.astype(jnp.bfloat16).reshape(4, 128, 128)

    each_unit(arrived, add_tiles, lambda n: all_three(lambda d: second(n, d).start()))

    def add_first(u, p):
        total = asend[by_portion(p, first_of), u].astype(jnp.float32)
        for d in range(3):
            total = total + arecv[d, u].astype(jnp.float32)
        bsend[u] = total.astype(jnp.bfloat16)

    each_unit(
        lambda n: all_three(lambda d: second(n, d).wait_recv()),
        add_first,
        lambda n: all_three(lambda d: third(n, d).start()),
    )

    def add_second(u, p):
        total = bsend[u].astype(jnp.float32)
        for d in range(3):
            total = total + brecv[d, u].astype(jnp.float32)
        coadd = total / den[p]
        cfull[u] = coadd
        gath[by_portion(p, first_of), u] = coadd.astype(jnp.bfloat16)

    each_unit(
        lambda n: all_three(lambda d: third(n, d).wait_recv()),
        add_second,
        lambda n: all_three(lambda d: fourth(n, d).start()),
    )

    def kept(p):
        return pl.ds(pl.multiple_of(second_of[p] * 32, 32), 32)

    def to_owner(n):
        p, lo, hi = SEGMENTS[n]
        return pltpu.make_async_remote_copy(
            src_ref=cfull.at[pl.ds(lo, hi - lo), kept(p)],
            dst_ref=crecv.at[pl.ds(lo, hi - lo)],
            send_sem=sc.at[n],
            recv_sem=rc.at[n],
            device_id=swap[p - 1],
            device_id_type=MESH,
        )

    for n, (p, lo, hi) in enumerate(SEGMENTS):
        if p > 0:

            @pl.when(moved[p - 1])
            def _(n=n):
                to_owner(n).start()

    def own_last(n):
        p, lo, hi = SEGMENTS[n]
        return pltpu.make_async_copy(
            at_group(send4, None, 0, lo, hi),
            at_group(recv4, None, ring_of[p] * 2 + c, lo, hi),
            own4.at[n],
        )

    def last(n, k):
        p, lo, hi = SEGMENTS[n]
        unused, pos, core = partner(p, k)
        return pltpu.make_async_remote_copy(
            src_ref=at_group(send4, None, k, lo, hi),
            dst_ref=at_group(recv4, None, ring_of[p] * 2 + c, lo, hi),
            send_sem=s4.at[n, k - 1],
            recv_sem=r4.at[n, k - 1],
            device_id=on_ring(p, pos, core),
            device_id_type=MESH,
        )

    def templates_here(n):
        p, lo, hi = SEGMENTS[n]
        all_three(lambda d: fourth(n, d).wait_recv())

        @pl.loop(lo, hi)
        def _(u):
            gathf[u] = gath[:, u].reshape(64, 8, 128).astype(jnp.float32)

    def pick(n, g):
        p, lo, hi = SEGMENTS[n]

        @pl.loop(0, 8)
        def _(k):
            for pair in range(PG):
                at = g * 8 * TG + k * TG + 2 * pair
                one, two = rows_s[p, at], rows_s[p, at + 1]
                for u in range(lo, hi):
                    send4[g, k, u, 16 * pair : 16 * pair + 16, :] = jnp.concatenate(
                        [gathf[u, one], gathf[u, two]], axis=0
                    ).astype(jnp.bfloat16)

    for n in range(len(SEGMENTS)):
        templates_here(n)

        @pl.loop(0, GROUPS)
        def _(g, n=n):
            pick(n, g)

        @pl.loop(1, 8)
        def _(k, n=n):
            last(n, k).start()

        own_last(n).start()

    for n, (p, lo, hi) in enumerate(SEGMENTS):
        if p == 0:
            crecv[lo:hi] = cfull[lo:hi, kept(p)]
        else:

            @pl.when(moved[p - 1])
            def _(n=n):
                to_owner(n).wait()

            @pl.when(jnp.logical_not(moved[p - 1]))
            def _(p=p, lo=lo, hi=hi):
                crecv[lo:hi] = cfull[lo:hi, kept(p)]

    keep_coadd = pltpu.make_async_copy(crecv, coadd_hbm, out_sem.at[2])
    keep_coadd.start()

    for n in range(len(SEGMENTS)):
        own_last(n).wait()

    @pl.loop(1, 8)
    def _(k):
        for n in range(len(SEGMENTS)):
            last(n, k).wait()
        for n in SECOND_WAVE:
            first(n, None, k).wait_send()

        @pl.loop(0, GROUPS)
        def _(g):
            for n in FIRST_WAVE:
                first(n, g, k).wait_send()

    @pl.loop(1, 4)
    def _(d):
        for n in range(len(SEGMENTS)):
            second(n, d).wait_send()
            third(n, d).wait_send()
            fourth(n, d).wait_send()

    keep_warp.wait()
    keep_mband.wait()
    keep_coadd.wait()


def subtract(warp, mband, picked, ahead, coadd_units, diff, coadd, fmat, tbuf, hbuf):
    @pl.when(pl.program_id(0) == 0)
    def _():
        @pl.loop(0, NF)
        def _(j):
            fmat[j] = jnp.zeros((SIDE, SIDE), jnp.bfloat16)
            write_square(ahead[j], fmat.at[j])

        for u in range(8):
            for k in range(4):
                coadd[k, 8 * (u // 2) : 8 * (u // 2) + 8, 128 * (u % 2) : 128 * (u % 2) + 128] = (
                    coadd_units[u, 8 * k : 8 * k + 8]
                )

    @pl.loop(0, 2)
    def _(pair):
        rows = pl.ds(pl.multiple_of(pair * 16, 16), 16)
        for q in range(8):
            for i in range(2):
                for b in range(2):
                    upper = picked[0, q, 4 * i + b, rows, :].astype(jnp.float32)
                    lower = picked[0, q, 4 * i + 2 + b, rows, :].astype(jnp.float32)
                    at = 32 * q + 16 * i
                    cols = slice(128 * b, 128 * b + 128)
                    tbuf[at : at + 16, cols] = jnp.concatenate([upper[0:8], lower[0:8]], axis=0).astype(
                        jnp.bfloat16
                    )
                    tbuf[SIDE + at : SIDE + at + 16, cols] = jnp.concatenate(
                        [upper[8:16], lower[8:16]], axis=0
                    ).astype(jnp.bfloat16)
        for j in range(NF):
            filtered = jnp.dot(tbuf[...], fmat[j], preferred_element_type=jnp.float32).astype(jnp.bfloat16)
            for i in range(4):
                hbuf[i, 128 * j : 128 * j + 128, :] = filtered[128 * i : 128 * i + 128]
        for half in range(2):
            t = pair * 2 + half
            top = jnp.dot(mband[t, 16:160, :], hbuf[2 * half], preferred_element_type=jnp.float32)
            low = jnp.dot(mband[t, 0:144, :], hbuf[2 * half + 1], preferred_element_type=jnp.float32)
            diff[t, 0:112] = warp[t, 0:112] - top[0:112]
            diff[t, 112:144] = warp[t, 112:144] - (top[112:144] + low[0:32])
            diff[t, 144:256] = warp[t, 144:256] - low[32:144]


def shards(tiles, shift_int, shift_frac, tile_weight, tile_patch, al_coeff):
    ahead, back = factor_strips()
    smem = pl.BlockSpec(memory_space=pltpu.SMEM)
    hbm = pl.BlockSpec(memory_space=pl.ANY)
    bf16, f32, i32 = jnp.bfloat16, jnp.float32, jnp.int32
    dma = pltpu.SemaphoreType.DMA
    block = (GROUPS, 8, 8, RB, 128)
    warp, mband, picked, coadd_units = pl.pallas_call(
        exchange,
        out_shape=(
            jax.ShapeDtypeStruct((TILES_DEV, SIDE, SIDE), f32),
            jax.ShapeDtypeStruct((TILES_DEV, 160, 128 * NF), bf16),
            jax.ShapeDtypeStruct(block, bf16),
            jax.ShapeDtypeStruct((8, 32, 128), f32),
        ),
        in_specs=[hbm, smem, smem, smem, hbm, hbm, hbm, hbm, hbm],
        out_specs=(hbm, hbm, hbm, hbm),
        scratch_shapes=[
            pltpu.VMEM((TILES_DEV, SIDE, SIDE), bf16),
            pltpu.VMEM((TILES_DEV, SIDE, SIDE), f32),
            pltpu.VMEM(block, bf16),
            pltpu.VMEM(block, bf16),
            pltpu.VMEM((3, 512, 1024), bf16),
            pltpu.VMEM((4, 8, 128, 128), bf16),
            pltpu.VMEM((3, 8, 128, 128), bf16),
            pltpu.VMEM((8, 128, 128), bf16),
            pltpu.VMEM((3, 8, 128, 128), bf16),
            pltpu.VMEM((4, 8, 128, 128), bf16),
            pltpu.VMEM((8, 64, 8, 128), f32),
            pltpu.VMEM(block, bf16),
            pltpu.VMEM((8, 128, 128), f32),
            pltpu.VMEM((8, 32, 128), f32),
            pltpu.VMEM((48, 8, 128), f32),
            pltpu.VMEM((3, 128, 128), f32),
            pltpu.VMEM((2 * TILES_DEV, 8, 128), f32),
            pltpu.VMEM((TILES_DEV, 160, 128 * NF), bf16),
            pltpu.VMEM((4, SIDE, SIDE), bf16),
            pltpu.VMEM((16, 128), i32),
            pltpu.VMEM((16, 128), f32),
            pltpu.VMEM((NF, 8, 128), f32),
            pltpu.SMEM((3, 128), i32),
            pltpu.SMEM((2048,), i32),
            pltpu.SMEM((2048,), f32),
            dma((3, GROUPS, 7)),
            dma((3, GROUPS, 7)),
            dma((3, 7)),
            dma((3, 7)),
            dma((6, 3)),
            dma((6, 3)),
            dma((6, 3)),
            dma((6, 3)),
            dma((6, 3)),
            dma((6, 3)),
            dma((6, 7)),
            dma((6, 7)),
            dma((6,)),
            dma((6,)),
            dma((GROUPS,)),
            dma((5,)),
            dma((6, GROUPS)),
            dma((6,)),
            dma((3,)),
        ],
        compiler_params=pltpu.CompilerParams(
            collective_id=0, has_side_effects=True, vmem_limit_bytes=56 << 20
        ),
    )(
        tiles,
        shift_int.T,
        shift_frac.T,
        al_coeff,
        tile_patch,
        tile_weight,
        tile_patch.reshape(16, 128),
        tile_weight.reshape(16, 128),
        jnp.asarray(back),
    )
    per = TG // 4
    difference, coadd = pl.pallas_call(
        subtract,
        grid=(TILES_DEV // 4,),
        out_shape=(
            jax.ShapeDtypeStruct((TILES_DEV, SIDE, SIDE), f32),
            jax.ShapeDtypeStruct((4, 32, SIDE), f32),
        ),
        in_specs=[
            pl.BlockSpec((4, SIDE, SIDE), lambda i: (i, 0, 0)),
            pl.BlockSpec((4, 160, 128 * NF), lambda i: (i, 0, 0)),
            pl.BlockSpec((1, 8, 8, 32, 128), lambda i: (i // per, 0, 0, i % per, 0)),
            pl.BlockSpec((NF, 8, 128), lambda i: (0, 0, 0)),
            pl.BlockSpec((8, 32, 128), lambda i: (0, 0, 0)),
        ],
        out_specs=(
            pl.BlockSpec((4, SIDE, SIDE), lambda i: (i, 0, 0)),
            pl.BlockSpec((4, 32, SIDE), lambda i: (0, 0, 0)),
        ),
        scratch_shapes=[
            pltpu.VMEM((NF, SIDE, SIDE), bf16),
            pltpu.VMEM((2 * SIDE, SIDE), bf16),
            pltpu.VMEM((4, 128 * NF, SIDE), bf16),
        ],
        compiler_params=pltpu.CompilerParams(vmem_limit_bytes=60 << 20),
    )(warp, mband, picked, jnp.asarray(ahead), coadd_units)
    return coadd, difference


def solution(mesh):
    return jax.shard_map(
        shards,
        mesh=mesh,
        in_specs=(
            P(("visit", "sky"), None, None),
            P(("visit", "sky"), None),
            P(("visit", "sky"), None),
            P(),
            P(),
            P(("visit", "sky"), None),
        ),
        out_specs=(P("sky", "visit", None), P(("visit", "sky"), None, None)),
        check_vma=False,
    )
```

time: 69.1 us -> 63.9 us (0.925)
  local copies, waits for them, and re-layouts: 6.16 us -> 0 us
  Pallas kernels: 62 us -> 63 us
    unnamed x2 -> x0, local copies, waits for them, and re-layouts: 6.16 us -> none
    pallas_call x1 -> x2, Pallas kernels: 62 us -> 63 us  [the longest x1 52.6 us: shards(): pl.pallas_call(exchange, out_shape=(jax.ShapeDtypeStruct((TILES_DEV, SIDE...]
where the time goes in v3:
time: 63.9 us; the launch traced here: 63.6 us
  Pallas kernels  63 us (99%)
  between operations  0.64 us (1%)
    pallas_call x1, Pallas kernels, shards(): pl.pallas_call(exchange, out_shape=(jax.ShapeDtypeStruct((TILES_DEV, SIDE...  52.6 us
    pallas_call x1, Pallas kernels, shards(): pl.pallas_call(subtract, grid=(TILES_DEV // 4,), out_shape=(jax.ShapeDtyp...  10.5 us

profile of v3, /device:TPU:1, one launch (start us, length us, event | category | flops | bytes accessed | tf_op | source)
XLA Modules:
  0.0 63.6 jit_solution(13314793218015555380)
XLA Ops:
  0.6 52.6 %shard_map.95 = (f32[16,256,256]{2,1,0:T(8,128)}, bf16[16,160,768]{2,1,0:T(8,128)(2,1)}, bf16[2,8,8,64,128]{4,3,2,1,0:T(8,128)(2,1)}, f32[8,32,128]{2,1,0:T(8,128)}) custom-call(bf16[16,256,256]{2,1,0:T(8,128)(2,1)} %tiles_hbm.1, s32[2,16]{1,0:T(2,128)} %bitcast.6, f32[2,16]{1,0:T(2,128)} %bitcast.7, f32[16,10]{1,0:T(8,128)} %coeff_s.1, s32[2048]{0:T(1024)} %patch_1d.1, ...), custom_call_target="tpu_custom_call" | custom-call | tf_op jit(solution)/shard_map/pallas_call | solution.py:641
  53.2 10.5 %shard_map.96 = (f32[16,256,256]{2,1,0:T(8,128)}, f32[4,32,256]{2,1,0:T(8,128)}) custom-call(f32[16,256,256]{2,1,0:T(8,128)} %get-tuple-element.8.warp, bf16[16,160,768]{2,1,0:T(8,128)(2,1)} %get-tuple-element.9.mband, bf16[2,8,8,64,128]{4,3,2,1,0:T(8,128)(2,1)} %get-tuple-element.10.picked, f32[6,8,128]{2,1,0:T(8,128)} %constant.5.clone.ahead, ...), custom_call_target="tpu_custom_call" | custom-call | tf_op jit(solution)/shard_map/pallas_call | solution.py:712

commit v4 on v3

v4 whole, which is shorter than its diff:
```python
import functools
import math

import jax
import jax.numpy as jnp
import numpy as np
from jax import lax
from jax.experimental import pallas as pl
from jax.experimental.pallas import tpu as pltpu
from jax.sharding import PartitionSpec as P

MESH = pl.DeviceIdType.MESH
KHALF = 10
SIDE = 256
TILES_DEV = 16
SIGMAS = (1.0, 2.5, 5.0)
FACTORS = ((0, 0), (0, 1), (0, 2), (1, 0), (1, 1), (2, 0))
BASIS_ROWS = (0, 1, 0, 2, 0, 1, 3, 4, 3, 5)
BASIS_COLS = (0, 0, 1, 0, 2, 1, 3, 3, 4, 5)
NF = len(FACTORS)

UNITS = 8
WAVES = 3


def wrapped_diff():
    diff = np.arange(128)[None, :] - np.arange(8)[:, None]
    return ((diff + 64) % 128) - 64


def factor_strips():
    diff = wrapped_diff().astype(np.float64)
    reach = np.arange(-KHALF, KHALF + 1).astype(np.float64)
    ahead, back = [], []
    for sigma_index, power in FACTORS:
        sigma = SIGMAS[sigma_index]
        norm = np.sum(np.exp(-reach * reach / (2.0 * sigma * sigma)))
        for out, u in ((ahead, diff), (back, -diff)):
            value = np.exp(-u * u / (2.0 * sigma * sigma)) * (u / sigma) ** power / norm
            out.append(np.where(np.abs(u) <= KHALF, value, 0.0))
    return np.stack(ahead).astype(np.float32), np.stack(back).astype(np.float32)


def sinc(v):
    scaled = math.pi * jnp.where(v == 0.0, 1.0, v)
    return jnp.where(v == 0.0, 1.0, jnp.sin(scaled) / scaled)


def lanczos(offset):
    return jnp.where(jnp.abs(offset) < 3.0, sinc(offset) * sinc(offset / 3.0), 0.0)


def by_portion(p, values):
    return jnp.where(p == 0, values[0], jnp.where(p == 1, values[1], values[2]))


def toeplitz_blocks(strip):
    lane = lax.broadcasted_iota(jnp.int32, (8, 128), 1)
    rows = [strip if b == 0 else pltpu.roll(strip, 8 * b, 1) for b in range(16)]
    low = lane < 64
    zero = jnp.zeros_like(strip)
    left = [jnp.where(low, zero, rows[b]) for b in (0, 1)]
    right = [jnp.where(low, rows[b], zero) for b in (14, 15)]
    for b in (0, 1):
        rows[b] = jnp.where(low, rows[b], zero)
    for b in (14, 15):
        rows[b] = jnp.where(low, zero, rows[b])

    def pack(pair):
        return jnp.concatenate(pair, axis=0).astype(jnp.bfloat16)

    return [pack(rows[2 * i : 2 * i + 2]) for i in range(8)], pack(right), pack(left)


def write_square(strip, ref):
    diag, right, left = toeplitz_blocks(strip)
    for i in range(8):
        ref[16 * i : 16 * i + 16, 0:128] = diag[i]
        ref[128 + 16 * i : 144 + 16 * i, 128:256] = diag[i]
    ref[112:128, 128:256] = right
    ref[128:144, 0:128] = left


def exchange(
    tiles_hbm,
    whole_s,
    part_s,
    patch_2d,
    weight_2d,
    warp_hbm,
    recv4,
    coadd_hbm,
    tiles,
    warp,
    send1,
    recv1,
    sel,
    selt,
    asend,
    arecv,
    bsend,
    brecv,
    gath,
    spread,
    send4,
    cfull,
    crecv,
    hits,
    den,
    strips,
    rmat,
    patch_v,
    weight_v,
    wcol,
    s1,
    r1,
    sa,
    ra,
    sb,
    rb,
    sga,
    rga,
    s4,
    r4,
    sc,
    rc,
    in_sem,
    small_sem,
    own1,
    own4,
    out_sem,
):
    visit, sky = lax.axis_index("visit"), lax.axis_index("sky")
    y, c = lax.div(visit, 2), lax.rem(visit, 2)
    z, x = lax.div(sky, 4), lax.rem(sky, 4)

    def dev(y_, c_, z_, x_):
        return (y_ * 2 + c_, z_ * 4 + x_)

    ring_of = (y, z, x)
    first_of, second_of = (x, y, z), (z, x, y)

    def on_ring(p, pos, core):
        return (dev(pos, core, z, x), dev(y, core, pos, x), dev(y, core, z, pos))[p]

    def on_first(p, pos):
        return (dev(y, c, z, pos), dev(pos, c, z, x), dev(y, c, pos, x))[p]

    def on_second(p, pos):
        return (dev(y, c, pos, x), dev(y, c, z, pos), dev(pos, c, z, x))[p]

    def partner(p, k):
        d, core = lax.div(k, 2), lax.rem(c + lax.rem(k, 2), 2)
        return lax.rem(ring_of[p] + d, 4), lax.rem(ring_of[p] + 4 - d, 4), core

    swap = (dev(z, c, y, x), dev(x, c, z, y))
    moved = (y != z, y != x)

    def fetch(i):
        half = pl.ds(i * (TILES_DEV // 2), TILES_DEV // 2)
        return pltpu.make_async_copy(tiles_hbm.at[half], tiles.at[half], in_sem.at[i])

    small = [
        pltpu.make_async_copy(here, there, small_sem.at[i])
        for i, (here, there) in enumerate(
            (
                (weight_2d, weight_v),
                (patch_2d, patch_v),
            )
        )
    ]

    barrier = pltpu.get_barrier_semaphore()
    pl.semaphore_signal(barrier, inc=1, device_id=dev(y, 1 - c, z, x), device_id_type=MESH)
    for p in range(3):

        @pl.loop(2, 8)
        def _(k, p=p):
            pos, unused, core = partner(p, k)
            pl.semaphore_signal(barrier, inc=1, device_id=on_ring(p, pos, core), device_id_type=MESH)

    for i in range(2):

        @pl.when(moved[i])
        def _(i=i):
            pl.semaphore_signal(barrier, inc=1, device_id=swap[i], device_id_type=MESH)

    for i in range(2):
        fetch(i).start()
    for copy in small:
        copy.start()

    lane = lax.broadcasted_iota(jnp.int32, (8, 128), 1)
    down = lax.broadcasted_iota(jnp.int32, (8, 128), 0)
    reach = jnp.where(lane < 64, lane, lane - 128).astype(jnp.float32)
    reach = jnp.where((down & 1) == 0, reach, -reach)

    @pl.loop(0, 4)
    def _(i):
        shift = jnp.zeros((8, 128), jnp.float32)
        for r in range(8):
            t = i * 4 + r // 2
            value = whole_s[r % 2, t].astype(jnp.float32) + part_s[r % 2, t]
            shift = jnp.where(down == r, value, shift)
        taps = lanczos(reach - shift)
        for r in range(8):
            row = jnp.broadcast_to(taps[r : r + 1], (8, 128))
            strips[i * 8 + r] = pltpu.roll(row, 0, 1, stride=1, stride_axis=0)

    @pl.loop(0, 4)
    def _(j):
        rmat[j] = jnp.zeros((SIDE, SIDE), jnp.bfloat16)

    def own_first(p, u):
        return pltpu.make_async_copy(send1.at[ring_of[p] * 2 + c, u], recv1.at[0, u], own1.at[u])

    def first(p, u, k):
        pos, unused, core = partner(p, k)
        return pltpu.make_async_remote_copy(
            src_ref=send1.at[pos * 2 + core, u],
            dst_ref=recv1.at[k, u],
            send_sem=s1.at[u],
            recv_sem=r1.at[u],
            device_id=on_ring(p, pos, core),
            device_id_type=MESH,
        )

    def start_wave(w):
        for p in range(3):
            u = 3 * w + p
            if u < UNITS:

                @pl.loop(0, 8)
                def _(q, u=u):
                    for r in range(8):
                        row = pl.ds(32 * q + 8 * (u // 2) + r, TILES_DEV, stride=SIDE)
                        send1[q, u, :, 128 * r : 128 * r + 128] = (wcol[...] * warp[u % 2, row]).astype(
                            jnp.bfloat16
                        )

                @pl.loop(1, 8)
                def _(k, p=p, u=u):
                    first(p, u, k).start()

                own_first(p, u).start()

    fetch(0).wait()

    @pl.loop(0, TILES_DEV // 2)
    def _(pair):
        @pl.when(pair == TILES_DEV // 4)
        def _():
            fetch(1).wait()

        for half in range(2):
            t = pair * 2 + half
            write_square(strips[2 * t], rmat.at[2 * half])
            write_square(strips[2 * t + 1], rmat.at[2 * half + 1])
            rowpass = jnp.dot(
                tiles[t], rmat[2 * half + 1], preferred_element_type=jnp.float32
            ).astype(jnp.bfloat16)
            value = jnp.dot(rmat[2 * half], rowpass, preferred_element_type=jnp.float32)
            for b in range(2):
                warp[b, pl.ds(pl.multiple_of(t * SIDE, SIDE), SIDE), :] = value[:, 128 * b : 128 * b + 128]

    small[0].wait()
    mine_row = weight_v[pl.ds(visit * 2 + lax.div(sky, 8), 1), :]
    mine_row = pltpu.roll(jnp.broadcast_to(mine_row, (8, 128)), lax.rem(128 - lax.rem(sky, 8) * 16, 128), 1)
    diagonal = lax.broadcasted_iota(jnp.int32, (TILES_DEV, 128), 0) == lax.broadcasted_iota(
        jnp.int32, (TILES_DEV, 128), 1
    )
    one_each = jnp.where(diagonal, jnp.broadcast_to(mine_row[0:1], (TILES_DEV, 128)), 0.0)
    wcol[...] = jnp.broadcast_to(jnp.sum(one_each, axis=1, keepdims=True), (TILES_DEV, 128))

    pl.semaphore_wait(barrier, 19 + moved[0].astype(jnp.int32) + moved[1].astype(jnp.int32))
    start_wave(0)

    keep_warp = pltpu.make_async_copy(warp, warp_hbm, out_sem.at[0])
    keep_warp.start()
    for copy in small[1:]:
        copy.wait()

    line = lax.broadcasted_iota(jnp.int32, (1, 128), 1)
    for p in range(3):
        key = jnp.zeros((1, 128), jnp.int32)
        for k in range(8):
            unused, pos, core = partner(p, k)
            v, s = on_ring(p, pos, core)
            found = jnp.broadcast_to(patch_v[pl.ds(v * 2 + lax.div(s, 8), 1), :], (8, 128))
            found = pltpu.roll(found, lax.rem(128 + 16 * k - lax.rem(s, 8) * 16, 128), 1)
            key = jnp.where((line >> 4) == k, found[0:1], key)
        if p == 0:
            key = ((key >> 2) & 3) * 16 + (key >> 4) * 4 + (key & 3)
        hot = jnp.where(
            jnp.broadcast_to(key, (128, 128)) == lax.broadcasted_iota(jnp.int32, (128, 128), 0), 1.0, 0.0
        )
        sel[p] = hot[0:64].astype(jnp.bfloat16)
        selt[p] = hot.T.astype(jnp.bfloat16)

    start_wave(1)

    @pl.loop(0, 48)
    def _(n):
        p, second, k = lax.div(n, 16), lax.rem(lax.div(n, 4), 4), lax.rem(n, 4)
        owner = by_portion(p, (second * 4 + x, y * 4 + second, z * 4 + second))
        hit = jnp.where(patch_v[...] == owner * 4 + k, weight_v[...], 0.0)
        hits[n] = hit[0:8] + hit[8:16]

    weights = 1.0 + jnp.sum(jnp.sum(hits[...], axis=1), axis=1, keepdims=True)
    for p in range(3):
        den[p] = jnp.broadcast_to(weights[16 * p : 16 * p + 16], (16, 128))

    start_wave(2)

    def second(p, u, d):
        pos = lax.rem(first_of[p] + d, 4)
        return pltpu.make_async_remote_copy(
            src_ref=asend.at[pos, u],
            dst_ref=arecv.at[d - 1, u],
            send_sem=sa.at[u],
            recv_sem=ra.at[u],
            device_id=on_first(p, pos),
            device_id_type=MESH,
        )

    def third(p, u, d):
        return pltpu.make_async_remote_copy(
            src_ref=bsend.at[u],
            dst_ref=brecv.at[d - 1, u],
            send_sem=sb.at[u],
            recv_sem=rb.at[u],
            device_id=on_second(p, lax.rem(second_of[p] + d, 4)),
            device_id_type=MESH,
        )

    def fourth(p, u, d):
        mine = gath.at[first_of[p], u]
        return pltpu.make_async_remote_copy(
            src_ref=mine,
            dst_ref=mine,
            send_sem=sga.at[u],
            recv_sem=rga.at[u],
            device_id=on_first(p, lax.rem(first_of[p] + d, 4)),
            device_id_type=MESH,
        )

    def to_owner(p, u):
        return pltpu.make_async_remote_copy(
            src_ref=cfull.at[u, second_of[p]],
            dst_ref=crecv.at[u],
            send_sem=sc.at[u],
            recv_sem=rc.at[u],
            device_id=swap[p - 1],
            device_id_type=MESH,
        )

    def own_last(p, u):
        return pltpu.make_async_copy(send4.at[0, u], recv4.at[ring_of[p] * 2 + c, u], own4.at[u])

    def last(p, u, k):
        unused, pos, core = partner(p, k)
        return pltpu.make_async_remote_copy(
            src_ref=send4.at[k, u],
            dst_ref=recv4.at[ring_of[p] * 2 + c, u],
            send_sem=s4.at[u],
            recv_sem=r4.at[u],
            device_id=on_ring(p, pos, core),
            device_id_type=MESH,
        )

    def each_unit(w, before, body, after):
        @pl.loop(0, 3)
        def _(i):
            u = 3 * w + i

            @pl.when(u < UNITS)
            def _():
                for p in range(3):

                    @pl.when(i == p)
                    def _(p=p):
                        before(p, u)

                body(u, i)
                for p in range(3):

                    @pl.when(i == p)
                    def _(p=p):
                        after(p, u)

    def all_three(act):
        @pl.loop(1, 4)
        def _(d):
            act(d)

    def all_seven(act):
        @pl.loop(1, 8)
        def _(k):
            act(k)

    def await_bytes(ref, sem):
        pltpu.make_async_copy(ref, ref, sem).wait()

    def seven(ref, u):
        return ref.at[pl.ds(1, 7), u]

    def three(ref, u):
        return ref.at[pl.ds(0, 3), u]

    def tiles_here(p, u):
        own_first(p, u).wait()
        await_bytes(seven(recv1, u), r1.at[u])

    def add_tiles(u, p):
        total = jnp.dot(sel[p], recv1[:, u].reshape(128, 1024), preferred_element_type=jnp.float32)
        asend[:, u] = total.astype(jnp.bfloat16).reshape(4, 16, 1024)

    def add_first(u, p):
        total = asend[by_portion(p, first_of), u].astype(jnp.float32)
        for d in range(3):
            total = total + arecv[d, u].astype(jnp.float32)
        bsend[u] = total.astype(jnp.bfloat16)

    def add_second(u, p):
        total = bsend[u].astype(jnp.float32)
        for d in range(3):
            total = total + brecv[d, u].astype(jnp.float32)
        coadd = total / jnp.concatenate([den[p]] * 8, axis=1)
        for b in range(4):
            cfull[u, b] = coadd[4 * b : 4 * b + 4]
        gath[by_portion(p, first_of), u] = coadd.astype(jnp.bfloat16)

    def templates_out(p, u):
        all_three(lambda d: fourth(p, u, d).start())
        if p > 0:

            @pl.when(moved[p - 1])
            def _():
                to_owner(p, u).start()

    def pick(u, p):
        found = jnp.dot(
            selt[p, :, 0:64], gath[:, u].reshape(64, 1024), preferred_element_type=jnp.float32
        )
        for r in range(8):
            spread[pl.ds(r, 128, stride=8), :] = found[:, 128 * r : 128 * r + 128]
        send4[:, u] = spread[...].astype(jnp.bfloat16).reshape(8, 128, 128)

    def picks_out(p, u):
        all_seven(lambda k: last(p, u, k).start())
        own_last(p, u).start()

    @pl.loop(0, WAVES + 3)
    def _(step):
        @pl.when(step < WAVES)
        def _():
            each_unit(
                step, tiles_here, add_tiles, lambda p, u: all_three(lambda d: second(p, u, d).start())
            )

        @pl.when((step >= 1) & (step < WAVES + 1))
        def _():
            each_unit(
                step - 1,
                lambda p, u: await_bytes(three(arecv, u), ra.at[u]),
                add_first,
                lambda p, u: all_three(lambda d: third(p, u, d).start()),
            )

        @pl.when((step >= 2) & (step < WAVES + 2))
        def _():
            each_unit(
                step - 2,
                lambda p, u: await_bytes(three(brecv, u), rb.at[u]),
                add_second,
                templates_out,
            )

        @pl.when(step >= 3)
        def _():
            each_unit(
                step - 3,
                lambda p, u: await_bytes(three(gath, u), rga.at[u]),
                pick,
                picks_out,
            )

    for u in range(UNITS):
        p = u % 3
        if p == 0:
            crecv[u] = cfull[u, second_of[p]]
        else:

            @pl.when(moved[p - 1])
            def _(p=p, u=u):
                to_owner(p, u).wait()

            @pl.when(jnp.logical_not(moved[p - 1]))
            def _(p=p, u=u):
                crecv[u] = cfull[u, second_of[p]]

    keep_coadd = pltpu.make_async_copy(crecv, coadd_hbm, out_sem.at[2])
    keep_coadd.start()

    @pl.loop(0, UNITS)
    def _(u):
        own_last(0, u).wait()
        await_bytes(seven(recv4, u), r4.at[u])
        await_bytes(seven(send4, u), s4.at[u])
        await_bytes(seven(send1, u), s1.at[u])
        await_bytes(three(asend, u), sa.at[u])
        await_bytes(three(brecv, u), sb.at[u])
        await_bytes(three(gath, u), sga.at[u])

    keep_warp.wait()
    keep_coadd.wait()


def subtract(coeff_s, warp, picked, ahead, back, coadd_units, diff, coadd, fmat, mband, tbuf, hbuf):
    @pl.when(pl.program_id(0) == 0)
    def _():
        @pl.loop(0, NF)
        def _(j):
            fmat[j] = jnp.zeros((SIDE, SIDE), jnp.bfloat16)
            write_square(ahead[j], fmat.at[j])

        @pl.loop(0, UNITS // 2)
        def _(rb):
            down = lax.broadcasted_iota(jnp.int32, (8, 128), 0)
            for cb in range(2):
                unit = coadd_units[2 * rb + cb]
                for k in range(4):
                    rows = jnp.zeros((8, 128), jnp.float32)
                    for r in range(8):
                        row = jnp.broadcast_to(unit[k : k + 1, 128 * r : 128 * r + 128], (8, 128))
                        rows = jnp.where(down == r, row, rows)
                    coadd[k, pl.ds(pl.multiple_of(rb * 8, 8), 8), 128 * cb : 128 * cb + 128] = rows

    @pl.loop(0, 2)
    def _(pair):
        rows = pl.ds(pl.multiple_of(pair * 16, 16), 16)
        for q in range(8):
            for i in range(2):
                for b in range(2):
                    upper = picked[q, 4 * i + b, rows, :].astype(jnp.float32)
                    lower = picked[q, 4 * i + 2 + b, rows, :].astype(jnp.float32)
                    at = 32 * q + 16 * i
                    cols = slice(128 * b, 128 * b + 128)
                    tbuf[at : at + 16, cols] = jnp.concatenate([upper[0:8], lower[0:8]], axis=0).astype(
                        jnp.bfloat16
                    )
                    tbuf[SIDE + at : SIDE + at + 16, cols] = jnp.concatenate(
                        [upper[8:16], lower[8:16]], axis=0
                    ).astype(jnp.bfloat16)
        for half in range(2):
            t = pl.program_id(0) * 4 + pair * 2 + half
            for j in range(NF):
                strip = None
                for k in range(len(BASIS_COLS)):
                    if BASIS_COLS[k] == j:
                        term = coeff_s[t, k] * back[BASIS_ROWS[k]]
                        strip = term if strip is None else strip + term
                diag, right, left = toeplitz_blocks(strip)
                cols = slice(128 * j, 128 * j + 128)
                mband[half, 0:16, cols] = right
                for i in range(8):
                    mband[half, 16 + 16 * i : 32 + 16 * i, cols] = diag[i]
                mband[half, 144:160, cols] = left
        for j in range(NF):
            filtered = jnp.dot(tbuf[...], fmat[j], preferred_element_type=jnp.float32).astype(jnp.bfloat16)
            for i in range(4):
                hbuf[i, 128 * j : 128 * j + 128, :] = filtered[128 * i : 128 * i + 128]
        for half in range(2):
            t = pair * 2 + half
            top = jnp.dot(mband[half, 16:160, :], hbuf[2 * half], preferred_element_type=jnp.float32)
            low = jnp.dot(mband[half, 0:144, :], hbuf[2 * half + 1], preferred_element_type=jnp.float32)
            whole = jnp.concatenate([top[0:112], top[112:144] + low[0:32], low[32:144]], axis=0)
            for b in range(2):
                cols = slice(128 * b, 128 * b + 128)
                diff[t, :, cols] = warp[b, pl.ds(pl.multiple_of(t * SIDE, SIDE), SIDE), :] - whole[:, cols]


def shards(tiles, shift_int, shift_frac, tile_weight, tile_patch, al_coeff):
    ahead, back = factor_strips()
    smem = pl.BlockSpec(memory_space=pltpu.SMEM)
    hbm = pl.BlockSpec(memory_space=pl.ANY)
    bf16, f32, i32 = jnp.bfloat16, jnp.float32, jnp.int32
    dma = pltpu.SemaphoreType.DMA
    lanes = (8, UNITS, TILES_DEV, 1024)
    block = (8, UNITS, TILES_DEV * 8, 128)
    warp, picked, coadd_units = pl.pallas_call(
        exchange,
        out_shape=(
            jax.ShapeDtypeStruct((2, TILES_DEV * SIDE, 128), f32),
            jax.ShapeDtypeStruct(block, bf16),
            jax.ShapeDtypeStruct((UNITS, 4, 1024), f32),
        ),
        in_specs=[hbm, smem, smem, hbm, hbm],
        out_specs=(hbm, hbm, hbm),
        scratch_shapes=[
            pltpu.VMEM((TILES_DEV, SIDE, SIDE), bf16),
            pltpu.VMEM((2, TILES_DEV * SIDE, 128), f32),
            pltpu.VMEM(lanes, bf16),
            pltpu.VMEM(lanes, bf16),
            pltpu.VMEM((3, 64, 128), bf16),
            pltpu.VMEM((3, 128, 128), bf16),
            pltpu.VMEM((4, UNITS, 16, 1024), bf16),
            pltpu.VMEM((3, UNITS, 16, 1024), bf16),
            pltpu.VMEM((UNITS, 16, 1024), bf16),
            pltpu.VMEM((3, UNITS, 16, 1024), bf16),
            pltpu.VMEM((4, UNITS, 16, 1024), bf16),
            pltpu.VMEM((1024, 128), f32),
            pltpu.VMEM(block, bf16),
            pltpu.VMEM((UNITS, 4, 4, 1024), f32),
            pltpu.VMEM((UNITS, 4, 1024), f32),
            pltpu.VMEM((48, 8, 128), f32),
            pltpu.VMEM((3, 16, 128), f32),
            pltpu.VMEM((2 * TILES_DEV, 8, 128), f32),
            pltpu.VMEM((4, SIDE, SIDE), bf16),
            pltpu.VMEM((16, 128), i32),
            pltpu.VMEM((16, 128), f32),
            pltpu.VMEM((TILES_DEV, 128), f32),
            dma((UNITS,)),
            dma((UNITS,)),
            dma((UNITS,)),
            dma((UNITS,)),
            dma((UNITS,)),
            dma((UNITS,)),
            dma((UNITS,)),
            dma((UNITS,)),
            dma((UNITS,)),
            dma((UNITS,)),
            dma((UNITS,)),
            dma((UNITS,)),
            dma((2,)),
            dma((2,)),
            dma((UNITS,)),
            dma((UNITS,)),
            dma((3,)),
        ],
        compiler_params=pltpu.CompilerParams(
            collective_id=0, has_side_effects=True, vmem_limit_bytes=56 << 20
        ),
    )(
        tiles,
        shift_int.T,
        shift_frac.T,
        tile_patch.reshape(16, 128),
        tile_weight.reshape(16, 128),
    )
    difference, coadd = pl.pallas_call(
        subtract,
        grid=(TILES_DEV // 4,),
        out_shape=(
            jax.ShapeDtypeStruct((TILES_DEV, SIDE, SIDE), f32),
            jax.ShapeDtypeStruct((4, 32, SIDE), f32),
        ),
        in_specs=[
            smem,
            pl.BlockSpec((2, 4 * SIDE, 128), lambda i: (0, i, 0)),
            pl.BlockSpec((8, UNITS, 32, 128), lambda i: (0, 0, i, 0)),
            pl.BlockSpec((NF, 8, 128), lambda i: (0, 0, 0)),
            pl.BlockSpec((NF, 8, 128), lambda i: (0, 0, 0)),
            pl.BlockSpec((UNITS, 4, 1024), lambda i: (0, 0, 0)),
        ],
        out_specs=(
            pl.BlockSpec((4, SIDE, SIDE), lambda i: (i, 0, 0)),
            pl.BlockSpec((4, 32, SIDE), lambda i: (0, 0, 0)),
        ),
        scratch_shapes=[
            pltpu.VMEM((NF, SIDE, SIDE), bf16),
            pltpu.VMEM((2, 160, 128 * NF), bf16),
            pltpu.VMEM((2 * SIDE, SIDE), bf16),
            pltpu.VMEM((4, 128 * NF, SIDE), bf16),
        ],
        compiler_params=pltpu.CompilerParams(vmem_limit_bytes=60 << 20),
    )(al_coeff, warp, picked, jnp.asarray(ahead), jnp.asarray(back), coadd_units)
    return coadd, difference


def solution(mesh):
    return jax.shard_map(
        shards,
        mesh=mesh,
        in_specs=(
            P(("visit", "sky"), None, None),
            P(("visit", "sky"), None),
            P(("visit", "sky"), None),
            P(),
            P(),
            P(("visit", "sky"), None),
        ),
        out_specs=(P("sky", "visit", None), P(("visit", "sky"), None, None)),
        check_vma=False,
    )
```

time: 63.9 us -> 60 us (0.939)
  Pallas kernels: 63 us -> 59.1 us
    pallas_call x1, Pallas kernels: 52.6 us -> 49.2 us  [shards(): pl.pallas_call(exchange, out_shape=(jax.ShapeDtypeStruct((2, TILES_DEV *...]
where the time goes in v4:
time: 60 us; the launch traced here: 59.8 us
  Pallas kernels  59.1 us (98%)
  between operations  0.64 us (1%)
    pallas_call x1, Pallas kernels, shards(): pl.pallas_call(exchange, out_shape=(jax.ShapeDtypeStruct((2, TILES_DEV *...  49.2 us
    pallas_call x1, Pallas kernels, shards(): pl.pallas_call(subtract, grid=(TILES_DEV // 4,), out_shape=(jax.ShapeDtyp...  9.89 us

profile of v4, /device:TPU:1, one launch (start us, length us, event | category | flops | bytes accessed | tf_op | source)
XLA Modules:
  0.0 59.8 jit_solution(1306517975992088740)
XLA Ops:
  0.6 49.2 %shard_map.95 = (f32[2,4096,128]{2,1,0:T(8,128)}, bf16[8,8,128,128]{3,2,1,0:T(8,128)(2,1)}, f32[8,4,1024]{2,1,0:T(4,128)}) custom-call(bf16[16,256,256]{2,1,0:T(8,128)(2,1)} %tiles_hbm.1, s32[2,16]{1,0:T(2,128)} %bitcast.6, f32[2,16]{1,0:T(2,128)} %bitcast.7, s32[16,128]{1,0:T(8,128)} %bitcast.4, f32[16,128]{1,0:T(8,128)} %bitcast.5), custom_call_target="tpu_custom_call" | custom-call | tf_op jit(solution)/shard_map/pallas_call | solution.py:591
  49.9 9.9 %shard_map.96 = (f32[16,256,256]{2,1,0:T(8,128)}, f32[4,32,256]{2,1,0:T(8,128)}) custom-call(f32[16,10]{1,0:T(8,128)} %coeff_s.1, f32[2,4096,128]{2,1,0:T(8,128)} %get-tuple-element.7.warp, bf16[8,8,128,128]{3,2,1,0:T(8,128)(2,1)} %get-tuple-element.8.picked, f32[6,8,128]{2,1,0:T(8,128)} %constant.4.clone.ahead, f32[6,8,128]{2,1,0:T(8,128)} %constant.5.clone.back, ...), custom_call_target="tpu_custom_call" | custom-call | tf_op jit(solution)/shard_map/pallas_call | solution.py:651

commit v5 on v4

--- a/solution.py
+++ b/solution.py
@@ -20,7 +20,7 @@
 NF = len(FACTORS)
 
 UNITS = 8
-WAVES = 3
+LAGS = (0, 5, 10, 15)
 
 
 def wrapped_diff():
@@ -83,8 +83,8 @@
 
 def exchange(
     tiles_hbm,
-    whole_s,
-    part_s,
+    whole_hbm,
+    part_hbm,
     patch_2d,
     weight_2d,
     warp_hbm,
@@ -105,6 +105,7 @@
     send4,
     cfull,
     crecv,
+    coadd,
     hits,
     den,
     strips,
@@ -112,6 +113,8 @@
     patch_v,
     weight_v,
     wcol,
+    whole_s,
+    part_s,
     s1,
     r1,
     sa,
@@ -166,6 +169,8 @@
             (
                 (weight_2d, weight_v),
                 (patch_2d, patch_v),
+                (whole_hbm, whole_s),
+                (part_hbm, part_s),
             )
         )
     ]
@@ -185,15 +190,18 @@
         def _(i=i):
             pl.semaphore_signal(barrier, inc=1, device_id=swap[i], device_id_type=MESH)
 
+    for copy in small:
+        copy.start()
     for i in range(2):
         fetch(i).start()
-    for copy in small:
-        copy.start()
 
     lane = lax.broadcasted_iota(jnp.int32, (8, 128), 1)
     down = lax.broadcasted_iota(jnp.int32, (8, 128), 0)
     reach = jnp.where(lane < 64, lane, lane - 128).astype(jnp.float32)
     reach = jnp.where((down & 1) == 0, reach, -reach)
+
+    for copy in small[2:]:
+        copy.wait()
 
     @pl.loop(0, 4)
     def _(i):
@@ -277,8 +285,7 @@
 
     keep_warp = pltpu.make_async_copy(warp, warp_hbm, out_sem.at[0])
     keep_warp.start()
-    for copy in small[1:]:
-        copy.wait()
+    small[1].wait()
 
     line = lax.broadcasted_iota(jnp.int32, (1, 128), 1)
     for p in range(3):
@@ -368,25 +375,22 @@
             device_id_type=MESH,
         )
 
-    def each_unit(w, before, body, after):
-        @pl.loop(0, 3)
-        def _(i):
-            u = 3 * w + i
-
-            @pl.when(u < UNITS)
-            def _():
-                for p in range(3):
-
-                    @pl.when(i == p)
-                    def _(p=p):
-                        before(p, u)
-
-                body(u, i)
-                for p in range(3):
-
-                    @pl.when(i == p)
-                    def _(p=p):
-                        after(p, u)
+    def one_unit(u, before, body, after):
+        @pl.when((u >= 0) & (u < UNITS))
+        def _():
+            portion = lax.rem(u, 3)
+            for p in range(3):
+
+                @pl.when(portion == p)
+                def _(p=p):
+                    before(p, u)
+
+            body(u, portion)
+            for p in range(3):
+
+                @pl.when(portion == p)
+                def _(p=p):
+                    after(p, u)
 
     def all_three(act):
         @pl.loop(1, 4)
@@ -425,10 +429,10 @@
         total = bsend[u].astype(jnp.float32)
         for d in range(3):
             total = total + brecv[d, u].astype(jnp.float32)
-        coadd = total / jnp.concatenate([den[p]] * 8, axis=1)
+        total = total / jnp.concatenate([den[p]] * 8, axis=1)
         for b in range(4):
-            cfull[u, b] = coadd[4 * b : 4 * b + 4]
-        gath[by_portion(p, first_of), u] = coadd.astype(jnp.bfloat16)
+            cfull[u, b] = total[4 * b : 4 * b + 4]
+        gath[by_portion(p, first_of), u] = total.astype(jnp.bfloat16)
 
     def templates_out(p, u):
         all_three(lambda d: fourth(p, u, d).start())
@@ -450,40 +454,32 @@
         all_seven(lambda k: last(p, u, k).start())
         own_last(p, u).start()
 
-    @pl.loop(0, WAVES + 3)
+    @pl.loop(0, UNITS + LAGS[3])
     def _(step):
-        @pl.when(step < WAVES)
-        def _():
-            each_unit(
-                step, tiles_here, add_tiles, lambda p, u: all_three(lambda d: second(p, u, d).start())
-            )
-
-        @pl.when((step >= 1) & (step < WAVES + 1))
-        def _():
-            each_unit(
-                step - 1,
-                lambda p, u: await_bytes(three(arecv, u), ra.at[u]),
-                add_first,
-                lambda p, u: all_three(lambda d: third(p, u, d).start()),
-            )
-
-        @pl.when((step >= 2) & (step < WAVES + 2))
-        def _():
-            each_unit(
-                step - 2,
-                lambda p, u: await_bytes(three(brecv, u), rb.at[u]),
-                add_second,
-                templates_out,
-            )
-
-        @pl.when(step >= 3)
-        def _():
-            each_unit(
-                step - 3,
-                lambda p, u: await_bytes(three(gath, u), rga.at[u]),
-                pick,
-                picks_out,
-            )
+        one_unit(
+            step - LAGS[0],
+            tiles_here,
+            add_tiles,
+            lambda p, u: all_three(lambda d: second(p, u, d).start()),
+        )
+        one_unit(
+            step - LAGS[1],
+            lambda p, u: await_bytes(three(arecv, u), ra.at[u]),
+            add_first,
+            lambda p, u: all_three(lambda d: third(p, u, d).start()),
+        )
+        one_unit(
+            step - LAGS[2],
+            lambda p, u: await_bytes(three(brecv, u), rb.at[u]),
+            add_second,
+            templates_out,
+        )
+        one_unit(
+            step - LAGS[3],
+            lambda p, u: await_bytes(three(gath, u), rga.at[u]),
+            pick,
+            picks_out,
+        )
 
     for u in range(UNITS):
         p = u % 3
@@ -499,7 +495,18 @@
             def _(p=p, u=u):
                 crecv[u] = cfull[u, second_of[p]]
 
-    keep_coadd = pltpu.make_async_copy(crecv, coadd_hbm, out_sem.at[2])
+    @pl.loop(0, UNITS // 2)
+    def _(rb):
+        for cb in range(2):
+            unit = crecv[2 * rb + cb]
+            for k in range(4):
+                rows = jnp.zeros((8, 128), jnp.float32)
+                for r in range(8):
+                    row = jnp.broadcast_to(unit[k : k + 1, 128 * r : 128 * r + 128], (8, 128))
+                    rows = jnp.where(down == r, row, rows)
+                coadd[k, pl.ds(pl.multiple_of(rb * 8, 8), 8), 128 * cb : 128 * cb + 128] = rows
+
+    keep_coadd = pltpu.make_async_copy(coadd, coadd_hbm, out_sem.at[2])
     keep_coadd.start()
 
     @pl.loop(0, UNITS)
@@ -516,28 +523,66 @@
     keep_coadd.wait()
 
 
-def subtract(coeff_s, warp, picked, ahead, back, coadd_units, diff, coadd, fmat, mband, tbuf, hbuf):
-    @pl.when(pl.program_id(0) == 0)
-    def _():
-        @pl.loop(0, NF)
-        def _(j):
-            fmat[j] = jnp.zeros((SIDE, SIDE), jnp.bfloat16)
-            write_square(ahead[j], fmat.at[j])
-
-        @pl.loop(0, UNITS // 2)
-        def _(rb):
-            down = lax.broadcasted_iota(jnp.int32, (8, 128), 0)
-            for cb in range(2):
-                unit = coadd_units[2 * rb + cb]
-                for k in range(4):
-                    rows = jnp.zeros((8, 128), jnp.float32)
-                    for r in range(8):
-                        row = jnp.broadcast_to(unit[k : k + 1, 128 * r : 128 * r + 128], (8, 128))
-                        rows = jnp.where(down == r, row, rows)
-                    coadd[k, pl.ds(pl.multiple_of(rb * 8, 8), 8), 128 * cb : 128 * cb + 128] = rows
-
-    @pl.loop(0, 2)
+def subtract(
+    coeff_s,
+    ahead_hbm,
+    back_hbm,
+    warp_hbm,
+    picked_hbm,
+    coadd_in,
+    diff_hbm,
+    coadd_out,
+    ahead,
+    back,
+    warp,
+    picked,
+    diff,
+    fmat,
+    mband,
+    tbuf,
+    hbuf,
+    strip_sem,
+    in_sem,
+    out_sem,
+    coadd_sem,
+):
+    pairs = TILES_DEV // 2
+
+    def enter(pair):
+        chunk = (slice(None), slice(None), pl.ds(pair * 16, 16))
+        rows = (slice(None), pl.ds(pair * 2 * SIDE, 2 * SIDE))
+        return (
+            pltpu.make_async_copy(picked_hbm.at[chunk], picked.at[chunk], in_sem.at[pair, 0]),
+            pltpu.make_async_copy(warp_hbm.at[rows], warp.at[rows], in_sem.at[pair, 1]),
+        )
+
+    def leave(pair):
+        here = pl.ds(pair * 2, 2)
+        return pltpu.make_async_copy(diff.at[here], diff_hbm.at[here], out_sem.at[pair])
+
+    strip_copies = (
+        pltpu.make_async_copy(ahead_hbm, ahead, strip_sem.at[0]),
+        pltpu.make_async_copy(back_hbm, back, strip_sem.at[1]),
+    )
+    for copy in strip_copies:
+        copy.start()
+
+    @pl.loop(0, pairs)
     def _(pair):
+        for copy in enter(pair):
+            copy.start()
+
+    pass_coadd = pltpu.make_async_copy(coadd_in, coadd_out, coadd_sem)
+    pass_coadd.start()
+    for copy in strip_copies:
+        copy.wait()
+
+    @pl.loop(0, NF)
+    def _(j):
+        fmat[j] = jnp.zeros((SIDE, SIDE), jnp.bfloat16)
+        write_square(ahead[j], fmat.at[j])
+
+    def assemble(pair, slot):
         rows = pl.ds(pl.multiple_of(pair * 16, 16), 16)
         for q in range(8):
             for i in range(2):
@@ -546,14 +591,16 @@
                     lower = picked[q, 4 * i + 2 + b, rows, :].astype(jnp.float32)
                     at = 32 * q + 16 * i
                     cols = slice(128 * b, 128 * b + 128)
-                    tbuf[at : at + 16, cols] = jnp.concatenate([upper[0:8], lower[0:8]], axis=0).astype(
-                        jnp.bfloat16
-                    )
-                    tbuf[SIDE + at : SIDE + at + 16, cols] = jnp.concatenate(
+                    tbuf[slot, at : at + 16, cols] = jnp.concatenate(
+                        [upper[0:8], lower[0:8]], axis=0
+                    ).astype(jnp.bfloat16)
+                    tbuf[slot, SIDE + at : SIDE + at + 16, cols] = jnp.concatenate(
                         [upper[8:16], lower[8:16]], axis=0
                     ).astype(jnp.bfloat16)
+
+    def mix(pair, slot):
         for half in range(2):
-            t = pl.program_id(0) * 4 + pair * 2 + half
+            t = pair * 2 + half
             for j in range(NF):
                 strip = None
                 for k in range(len(BASIS_COLS)):
@@ -562,22 +609,48 @@
                         strip = term if strip is None else strip + term
                 diag, right, left = toeplitz_blocks(strip)
                 cols = slice(128 * j, 128 * j + 128)
-                mband[half, 0:16, cols] = right
+                mband[slot, half, 0:16, cols] = right
                 for i in range(8):
-                    mband[half, 16 + 16 * i : 32 + 16 * i, cols] = diag[i]
-                mband[half, 144:160, cols] = left
+                    mband[slot, half, 16 + 16 * i : 32 + 16 * i, cols] = diag[i]
+                mband[slot, half, 144:160, cols] = left
+
+    def columns(slot):
         for j in range(NF):
-            filtered = jnp.dot(tbuf[...], fmat[j], preferred_element_type=jnp.float32).astype(jnp.bfloat16)
+            filtered = jnp.dot(tbuf[slot], fmat[j], preferred_element_type=jnp.float32).astype(jnp.bfloat16)
             for i in range(4):
-                hbuf[i, 128 * j : 128 * j + 128, :] = filtered[128 * i : 128 * i + 128]
+                hbuf[slot, i, 128 * j : 128 * j + 128, :] = filtered[128 * i : 128 * i + 128]
+
+    def rest(pair, slot):
         for half in range(2):
             t = pair * 2 + half
-            top = jnp.dot(mband[half, 16:160, :], hbuf[2 * half], preferred_element_type=jnp.float32)
-            low = jnp.dot(mband[half, 0:144, :], hbuf[2 * half + 1], preferred_element_type=jnp.float32)
+            top = jnp.dot(mband[slot, half, 16:160, :], hbuf[slot, 2 * half], preferred_element_type=jnp.float32)
+            low = jnp.dot(
+                mband[slot, half, 0:144, :], hbuf[slot, 2 * half + 1], preferred_element_type=jnp.float32
+            )
             whole = jnp.concatenate([top[0:112], top[112:144] + low[0:32], low[32:144]], axis=0)
             for b in range(2):
                 cols = slice(128 * b, 128 * b + 128)
                 diff[t, :, cols] = warp[b, pl.ds(pl.multiple_of(t * SIDE, SIDE), SIDE), :] - whole[:, cols]
+        leave(pair).start()
+
+    @pl.loop(0, pairs // 2)
+    def _(step):
+        chosen = [step * 2 + slot for slot in range(2)]
+        for pair in chosen:
+            for copy in enter(pair):
+                copy.wait()
+        for slot, pair in enumerate(chosen):
+            assemble(pair, slot)
+            mix(pair, slot)
+            columns(slot)
+        for slot, pair in enumerate(chosen):
+            rest(pair, slot)
+
+    @pl.loop(0, pairs)
+    def _(pair):
+        leave(pair).wait()
+
+    pass_coadd.wait()
 
 
 def shards(tiles, shift_int, shift_frac, tile_weight, tile_patch, al_coeff):
@@ -593,9 +666,9 @@
         out_shape=(
             jax.ShapeDtypeStruct((2, TILES_DEV * SIDE, 128), f32),
             jax.ShapeDtypeStruct(block, bf16),
-            jax.ShapeDtypeStruct((UNITS, 4, 1024), f32),
+            jax.ShapeDtypeStruct((4, 32, SIDE), f32),
         ),
-        in_specs=[hbm, smem, smem, hbm, hbm],
+        in_specs=[hbm, hbm, hbm, hbm, hbm],
         out_specs=(hbm, hbm, hbm),
         scratch_shapes=[
             pltpu.VMEM((TILES_DEV, SIDE, SIDE), bf16),
@@ -613,6 +686,7 @@
             pltpu.VMEM(block, bf16),
             pltpu.VMEM((UNITS, 4, 4, 1024), f32),
             pltpu.VMEM((UNITS, 4, 1024), f32),
+            pltpu.VMEM((4, 32, SIDE), f32),
             pltpu.VMEM((48, 8, 128), f32),
             pltpu.VMEM((3, 16, 128), f32),
             pltpu.VMEM((2 * TILES_DEV, 8, 128), f32),
@@ -620,6 +694,8 @@
             pltpu.VMEM((16, 128), i32),
             pltpu.VMEM((16, 128), f32),
             pltpu.VMEM((TILES_DEV, 128), f32),
+            pltpu.SMEM((2, TILES_DEV), i32),
+            pltpu.SMEM((2, TILES_DEV), f32),
             dma((UNITS,)),
             dma((UNITS,)),
             dma((UNITS,)),
@@ -633,7 +709,7 @@
             dma((UNITS,)),
             dma((UNITS,)),
             dma((2,)),
-            dma((2,)),
+            dma((4,)),
             dma((UNITS,)),
             dma((UNITS,)),
             dma((3,)),
@@ -650,31 +726,29 @@
     )
     difference, coadd = pl.pallas_call(
         subtract,
-        grid=(TILES_DEV // 4,),
         out_shape=(
             jax.ShapeDtypeStruct((TILES_DEV, SIDE, SIDE), f32),
             jax.ShapeDtypeStruct((4, 32, SIDE), f32),
         ),
-        in_specs=[
-            smem,
-            pl.BlockSpec((2, 4 * SIDE, 128), lambda i: (0, i, 0)),
-            pl.BlockSpec((8, UNITS, 32, 128), lambda i: (0, 0, i, 0)),
-            pl.BlockSpec((NF, 8, 128), lambda i: (0, 0, 0)),
-            pl.BlockSpec((NF, 8, 128), lambda i: (0, 0, 0)),
-            pl.BlockSpec((UNITS, 4, 1024), lambda i: (0, 0, 0)),
-        ],
-        out_specs=(
-            pl.BlockSpec((4, SIDE, SIDE), lambda i: (i, 0, 0)),
-            pl.BlockSpec((4, 32, SIDE), lambda i: (0, 0, 0)),
-        ),
+        in_specs=[smem, hbm, hbm, hbm, hbm, hbm],
+        out_specs=(hbm, hbm),
         scratch_shapes=[
+            pltpu.VMEM((NF, 8, 128), f32),
+            pltpu.VMEM((NF, 8, 128), f32),
+            pltpu.VMEM((2, TILES_DEV * SIDE, 128), f32),
+            pltpu.VMEM(block, bf16),
+            pltpu.VMEM((TILES_DEV, SIDE, SIDE), f32),
             pltpu.VMEM((NF, SIDE, SIDE), bf16),
-            pltpu.VMEM((2, 160, 128 * NF), bf16),
-            pltpu.VMEM((2 * SIDE, SIDE), bf16),
-            pltpu.VMEM((4, 128 * NF, SIDE), bf16),
+            pltpu.VMEM((2, 2, 160, 128 * NF), bf16),
+            pltpu.VMEM((2, 2 * SIDE, SIDE), bf16),
+            pltpu.VMEM((2, 4, 128 * NF, SIDE), bf16),
+            dma((2,)),
+            dma((TILES_DEV // 2, 2)),
+            dma((TILES_DEV // 2,)),
+            dma,
         ],
         compiler_params=pltpu.CompilerParams(vmem_limit_bytes=60 << 20),
-    )(al_coeff, warp, picked, jnp.asarray(ahead), jnp.asarray(back), coadd_units)
+    )(al_coeff, jnp.asarray(ahead), jnp.asarray(back), warp, picked, coadd_units)
     return coadd, difference
 
 

time: 60 us -> 57.8 us (0.963)
  Pallas kernels: 59.1 us -> 56.9 us
    pallas_call x1, Pallas kernels: 49.2 us -> 47.6 us  [shards(): pl.pallas_call(exchange, out_shape=(jax.ShapeDtypeStruct((2, TILES_DEV *...]
where the time goes in v5:
time: 57.8 us; the launch traced here: 57.6 us
  Pallas kernels  56.9 us (98%)
  between operations  0.64 us (1%)
    pallas_call x1, Pallas kernels, shards(): pl.pallas_call(exchange, out_shape=(jax.ShapeDtypeStruct((2, TILES_DEV *...  47.6 us
    pallas_call x1, Pallas kernels, shards(): pl.pallas_call(subtract, out_shape=(jax.ShapeDtypeStruct((TILES_DEV, SIDE...  9.31 us

profile of v5, /device:TPU:1, one launch (start us, length us, event | category | flops | bytes accessed | tf_op | source)
XLA Modules:
  0.0 57.6 jit_solution(18360116629631761394)
XLA Ops:
  0.6 47.6 %shard_map.95 = (f32[2,4096,128]{2,1,0:T(8,128)}, bf16[8,8,128,128]{3,2,1,0:T(8,128)(2,1)}, f32[4,32,256]{2,1,0:T(8,128)}) custom-call(bf16[16,256,256]{2,1,0:T(8,128)(2,1)} %tiles_hbm.1, s32[2,16]{1,0:T(2,128)} %bitcast.6, f32[2,16]{1,0:T(2,128)} %bitcast.7, s32[16,128]{1,0:T(8,128)} %bitcast.4, f32[16,128]{1,0:T(8,128)} %bitcast.5), custom_call_target="tpu_custom_call" | custom-call | tf_op jit(solution)/shard_map/pallas_call | solution.py:664
  48.3 9.3 %shard_map.96 = (f32[16,256,256]{2,1,0:T(8,128)}, f32[4,32,256]{2,1,0:T(8,128)}) custom-call(f32[16,10]{1,0:T(8,128)} %coeff_s.1, f32[6,8,128]{2,1,0:T(8,128)} %constant.4.clone.ahead_hbm, f32[6,8,128]{2,1,0:T(8,128)} %constant.5.clone.back_hbm, f32[2,4096,128]{2,1,0:T(8,128)} %get-tuple-element.7.warp_hbm, ...), custom_call_target="tpu_custom_call" | custom-call | tf_op jit(solution)/shard_map/pallas_call | solution.py:727

commit v6 on v5

--- a/solution.py
+++ b/solution.py
@@ -215,7 +215,7 @@
             row = jnp.broadcast_to(taps[r : r + 1], (8, 128))
             strips[i * 8 + r] = pltpu.roll(row, 0, 1, stride=1, stride_axis=0)
 
-    @pl.loop(0, 4)
+    @pl.loop(0, 16)
     def _(j):
         rmat[j] = jnp.zeros((SIDE, SIDE), jnp.bfloat16)
 
@@ -254,22 +254,27 @@
 
     fetch(0).wait()
 
-    @pl.loop(0, TILES_DEV // 2)
-    def _(pair):
-        @pl.when(pair == TILES_DEV // 4)
+    @pl.loop(0, TILES_DEV // 8)
+    def _(octet):
+        @pl.when(octet == TILES_DEV // 16)
         def _():
             fetch(1).wait()
 
-        for half in range(2):
-            t = pair * 2 + half
-            write_square(strips[2 * t], rmat.at[2 * half])
-            write_square(strips[2 * t + 1], rmat.at[2 * half + 1])
-            rowpass = jnp.dot(
-                tiles[t], rmat[2 * half + 1], preferred_element_type=jnp.float32
-            ).astype(jnp.bfloat16)
-            value = jnp.dot(rmat[2 * half], rowpass, preferred_element_type=jnp.float32)
+        for i in range(8):
+            t = octet * 8 + i
+            write_square(strips[2 * t], rmat.at[2 * i])
+            write_square(strips[2 * t + 1], rmat.at[2 * i + 1])
+        rowpasses = [
+            jnp.dot(tiles[octet * 8 + i], rmat[2 * i + 1], preferred_element_type=jnp.float32).astype(
+                jnp.bfloat16
+            )
+            for i in range(8)
+        ]
+        for i in range(8):
+            value = jnp.dot(rmat[2 * i], rowpasses[i], preferred_element_type=jnp.float32)
+            rows = pl.ds(pl.multiple_of((octet * 8 + i) * SIDE, SIDE), SIDE)
             for b in range(2):
-                warp[b, pl.ds(pl.multiple_of(t * SIDE, SIDE), SIDE), :] = value[:, 128 * b : 128 * b + 128]
+                warp[b, rows, :] = value[:, 128 * b : 128 * b + 128]
 
     small[0].wait()
     mine_row = weight_v[pl.ds(visit * 2 + lax.div(sky, 8), 1), :]
@@ -690,7 +695,7 @@
             pltpu.VMEM((48, 8, 128), f32),
             pltpu.VMEM((3, 16, 128), f32),
             pltpu.VMEM((2 * TILES_DEV, 8, 128), f32),
-            pltpu.VMEM((4, SIDE, SIDE), bf16),
+            pltpu.VMEM((16, SIDE, SIDE), bf16),
             pltpu.VMEM((16, 128), i32),
             pltpu.VMEM((16, 128), f32),
             pltpu.VMEM((TILES_DEV, 128), f32),

time: 57.8 us -> 55 us (0.952)
  Pallas kernels: 56.9 us -> 54.2 us
    pallas_call x1, Pallas kernels: 47.6 us -> 44.9 us  [shards(): pl.pallas_call(exchange, out_shape=(jax.ShapeDtypeStruct((2, TILES_DEV *...]
where the time goes in v6:
time: 55 us; the launch traced here: 54.9 us
  Pallas kernels  54.2 us (99%)
  between operations  0.64 us (1%)
    pallas_call x1, Pallas kernels, shards(): pl.pallas_call(exchange, out_shape=(jax.ShapeDtypeStruct((2, TILES_DEV *...  44.9 us
    pallas_call x1, Pallas kernels, shards(): pl.pallas_call(subtract, out_shape=(jax.ShapeDtypeStruct((TILES_DEV, SIDE...  9.32 us

profile of v6, /device:TPU:1, one launch (start us, length us, event | category | flops | bytes accessed | tf_op | source)
XLA Modules:
  0.0 54.9 jit_solution(7716797051629978295)
XLA Ops:
  0.6 44.9 %shard_map.95 = (f32[2,4096,128]{2,1,0:T(8,128)}, bf16[8,8,128,128]{3,2,1,0:T(8,128)(2,1)}, f32[4,32,256]{2,1,0:T(8,128)}) custom-call(bf16[16,256,256]{2,1,0:T(8,128)(2,1)} %tiles_hbm.1, s32[2,16]{1,0:T(2,128)} %bitcast.6, f32[2,16]{1,0:T(2,128)} %bitcast.7, s32[16,128]{1,0:T(8,128)} %bitcast.4, f32[16,128]{1,0:T(8,128)} %bitcast.5), custom_call_target="tpu_custom_call" | custom-call | tf_op jit(solution)/shard_map/pallas_call | solution.py:669
  45.5 9.3 %shard_map.96 = (f32[16,256,256]{2,1,0:T(8,128)}, f32[4,32,256]{2,1,0:T(8,128)}) custom-call(f32[16,10]{1,0:T(8,128)} %coeff_s.1, f32[6,8,128]{2,1,0:T(8,128)} %constant.4.clone.ahead_hbm, f32[6,8,128]{2,1,0:T(8,128)} %constant.5.clone.back_hbm, f32[2,4096,128]{2,1,0:T(8,128)} %get-tuple-element.7.warp_hbm, ...), custom_call_target="tpu_custom_call" | custom-call | tf_op jit(solution)/shard_map/pallas_call | solution.py:732

commit v7 on v6

--- a/solution.py
+++ b/solution.py
@@ -200,11 +200,14 @@
     reach = jnp.where(lane < 64, lane, lane - 128).astype(jnp.float32)
     reach = jnp.where((down & 1) == 0, reach, -reach)
 
+    @pl.loop(0, 16)
+    def _(j):
+        rmat[j] = jnp.zeros((SIDE, SIDE), jnp.bfloat16)
+
     for copy in small[2:]:
         copy.wait()
 
-    @pl.loop(0, 4)
-    def _(i):
+    for i in range(4):
         shift = jnp.zeros((8, 128), jnp.float32)
         for r in range(8):
             t = i * 4 + r // 2
@@ -214,10 +217,6 @@
         for r in range(8):
             row = jnp.broadcast_to(taps[r : r + 1], (8, 128))
             strips[i * 8 + r] = pltpu.roll(row, 0, 1, stride=1, stride_axis=0)
-
-    @pl.loop(0, 16)
-    def _(j):
-        rmat[j] = jnp.zeros((SIDE, SIDE), jnp.bfloat16)
 
     def own_first(p, u):
         return pltpu.make_async_copy(send1.at[ring_of[p] * 2 + c, u], recv1.at[0, u], own1.at[u])

time: 55 us -> 54.8 us (level)
  no operation moved by 1% of the time
where the time goes in v7:
time: 54.8 us; the launch traced here: 54.6 us
  Pallas kernels  54 us (99%)
  between operations  0.64 us (1%)
    pallas_call x1, Pallas kernels, shards(): pl.pallas_call(exchange, out_shape=(jax.ShapeDtypeStruct((2, TILES_DEV *...  44.7 us
    pallas_call x1, Pallas kernels, shards(): pl.pallas_call(subtract, out_shape=(jax.ShapeDtypeStruct((TILES_DEV, SIDE...  9.31 us

profile of v7, /device:TPU:1, one launch (start us, length us, event | category | flops | bytes accessed | tf_op | source)
XLA Modules:
  0.0 54.6 jit_solution(9535369298247510660)
XLA Ops:
  0.6 44.7 %shard_map.95 = (f32[2,4096,128]{2,1,0:T(8,128)}, bf16[8,8,128,128]{3,2,1,0:T(8,128)(2,1)}, f32[4,32,256]{2,1,0:T(8,128)}) custom-call(bf16[16,256,256]{2,1,0:T(8,128)(2,1)} %tiles_hbm.1, s32[2,16]{1,0:T(2,128)} %bitcast.6, f32[2,16]{1,0:T(2,128)} %bitcast.7, s32[16,128]{1,0:T(8,128)} %bitcast.4, f32[16,128]{1,0:T(8,128)} %bitcast.5), custom_call_target="tpu_custom_call" | custom-call | tf_op jit(solution)/shard_map/pallas_call | solution.py:668
  45.3 9.3 %shard_map.96 = (f32[16,256,256]{2,1,0:T(8,128)}, f32[4,32,256]{2,1,0:T(8,128)}) custom-call(f32[16,10]{1,0:T(8,128)} %coeff_s.1, f32[6,8,128]{2,1,0:T(8,128)} %constant.4.clone.ahead_hbm, f32[6,8,128]{2,1,0:T(8,128)} %constant.5.clone.back_hbm, f32[2,4096,128]{2,1,0:T(8,128)} %get-tuple-element.7.warp_hbm, ...), custom_call_target="tpu_custom_call" | custom-call | tf_op jit(solution)/shard_map/pallas_call | solution.py:731

commit v8 on v7

--- a/solution.py
+++ b/solution.py
@@ -87,9 +87,11 @@
     part_hbm,
     patch_2d,
     weight_2d,
+    ahead_hbm,
     warp_hbm,
     recv4,
     coadd_hbm,
+    fmat_hbm,
     tiles,
     warp,
     send1,
@@ -113,6 +115,8 @@
     patch_v,
     weight_v,
     wcol,
+    ahead,
+    fmat,
     whole_s,
     part_s,
     s1,
@@ -171,6 +175,7 @@
                 (patch_2d, patch_v),
                 (whole_hbm, whole_s),
                 (part_hbm, part_s),
+                (ahead_hbm, ahead),
             )
         )
     ]
@@ -204,7 +209,7 @@
     def _(j):
         rmat[j] = jnp.zeros((SIDE, SIDE), jnp.bfloat16)
 
-    for copy in small[2:]:
+    for copy in small[2:4]:
         copy.wait()
 
     for i in range(4):
@@ -323,6 +328,16 @@
 
     start_wave(2)
 
+    small[4].wait()
+
+    @pl.loop(0, NF)
+    def _(j):
+        fmat[j] = jnp.zeros((SIDE, SIDE), jnp.bfloat16)
+        write_square(ahead[j], fmat.at[j])
+
+    keep_fmat = pltpu.make_async_copy(fmat, fmat_hbm, out_sem.at[1])
+    keep_fmat.start()
+
     def second(p, u, d):
         pos = lax.rem(first_of[p] + d, 4)
         return pltpu.make_async_remote_copy(
@@ -524,19 +539,19 @@
         await_bytes(three(gath, u), sga.at[u])
 
     keep_warp.wait()
+    keep_fmat.wait()
     keep_coadd.wait()
 
 
 def subtract(
     coeff_s,
-    ahead_hbm,
+    fmat_hbm,
     back_hbm,
     warp_hbm,
     picked_hbm,
     coadd_in,
     diff_hbm,
     coadd_out,
-    ahead,
     back,
     warp,
     picked,
@@ -565,7 +580,7 @@
         return pltpu.make_async_copy(diff.at[here], diff_hbm.at[here], out_sem.at[pair])
 
     strip_copies = (
-        pltpu.make_async_copy(ahead_hbm, ahead, strip_sem.at[0]),
+        pltpu.make_async_copy(fmat_hbm, fmat, strip_sem.at[0]),
         pltpu.make_async_copy(back_hbm, back, strip_sem.at[1]),
     )
     for copy in strip_copies:
@@ -580,11 +595,6 @@
     pass_coadd.start()
     for copy in strip_copies:
         copy.wait()
-
-    @pl.loop(0, NF)
-    def _(j):
-        fmat[j] = jnp.zeros((SIDE, SIDE), jnp.bfloat16)
-        write_square(ahead[j], fmat.at[j])
 
     def assemble(pair, slot):
         rows = pl.ds(pl.multiple_of(pair * 16, 16), 16)
@@ -665,15 +675,16 @@
     dma = pltpu.SemaphoreType.DMA
     lanes = (8, UNITS, TILES_DEV, 1024)
     block = (8, UNITS, TILES_DEV * 8, 128)
-    warp, picked, coadd_units = pl.pallas_call(
+    warp, picked, coadd_units, columns = pl.pallas_call(
         exchange,
         out_shape=(
             jax.ShapeDtypeStruct((2, TILES_DEV * SIDE, 128), f32),
             jax.ShapeDtypeStruct(block, bf16),
             jax.ShapeDtypeStruct((4, 32, SIDE), f32),
+            jax.ShapeDtypeStruct((NF, SIDE, SIDE), bf16),
         ),
-        in_specs=[hbm, hbm, hbm, hbm, hbm],
-        out_specs=(hbm, hbm, hbm),
+        in_specs=[hbm] * 6,
+        out_specs=(hbm, hbm, hbm, hbm),
         scratch_shapes=[
             pltpu.VMEM((TILES_DEV, SIDE, SIDE), bf16),
             pltpu.VMEM((2, TILES_DEV * SIDE, 128), f32),
@@ -698,6 +709,8 @@
             pltpu.VMEM((16, 128), i32),
             pltpu.VMEM((16, 128), f32),
             pltpu.VMEM((TILES_DEV, 128), f32),
+            pltpu.VMEM((NF, 8, 128), f32),
+            pltpu.VMEM((NF, SIDE, SIDE), bf16),
             pltpu.SMEM((2, TILES_DEV), i32),
             pltpu.SMEM((2, TILES_DEV), f32),
             dma((UNITS,)),
@@ -713,7 +726,7 @@
             dma((UNITS,)),
             dma((UNITS,)),
             dma((2,)),
-            dma((4,)),
+            dma((5,)),
             dma((UNITS,)),
             dma((UNITS,)),
             dma((3,)),
@@ -727,6 +740,7 @@
         shift_frac.T,
         tile_patch.reshape(16, 128),
         tile_weight.reshape(16, 128),
+        jnp.asarray(ahead),
     )
     difference, coadd = pl.pallas_call(
         subtract,
@@ -737,7 +751,6 @@
         in_specs=[smem, hbm, hbm, hbm, hbm, hbm],
         out_specs=(hbm, hbm),
         scratch_shapes=[
-            pltpu.VMEM((NF, 8, 128), f32),
             pltpu.VMEM((NF, 8, 128), f32),
             pltpu.VMEM((2, TILES_DEV * SIDE, 128), f32),
             pltpu.VMEM(block, bf16),
@@ -752,7 +765,7 @@
             dma,
         ],
         compiler_params=pltpu.CompilerParams(vmem_limit_bytes=60 << 20),
-    )(al_coeff, jnp.asarray(ahead), jnp.asarray(back), warp, picked, coadd_units)
+    )(al_coeff, columns, jnp.asarray(back), warp, picked, coadd_units)
     return coadd, difference
 
 

time: 54.8 us -> 55.2 us (level)
  no operation moved by 1% of the time
where the time goes in v8:
time: 55.2 us; the launch traced here: 55 us
  Pallas kernels  54.4 us (99%)
  between operations  0.64 us (1%)
    pallas_call x1, Pallas kernels, shards(): pl.pallas_call(exchange, out_shape=(jax.ShapeDtypeStruct((2, TILES_DEV *...  44.7 us
    pallas_call x1, Pallas kernels, shards(): pl.pallas_call(subtract, out_shape=(jax.ShapeDtypeStruct((TILES_DEV, SIDE...  9.71 us

profile of v8, /device:TPU:1, one launch (start us, length us, event | category | flops | bytes accessed | tf_op | source)
XLA Modules:
  0.0 55.0 jit_solution(18342151834270861744)
XLA Ops:
  0.6 44.7 %shard_map.95 = (f32[2,4096,128]{2,1,0:T(8,128)}, bf16[8,8,128,128]{3,2,1,0:T(8,128)(2,1)}, f32[4,32,256]{2,1,0:T(8,128)}, bf16[6,256,256]{2,1,0:T(8,128)(2,1)}) custom-call(bf16[16,256,256]{2,1,0:T(8,128)(2,1)} %tiles_hbm.1, s32[2,16]{1,0:T(2,128)} %bitcast.6, f32[2,16]{1,0:T(2,128)} %bitcast.7, s32[16,128]{1,0:T(8,128)} %bitcast.4, f32[16,128]{1,0:T(8,128)} %bitcast.5, ...), custom_call_target="tpu_custom_call" | custom-call | tf_op jit(solution)/shard_map/pallas_call | solution.py:678
  45.3 9.7 %shard_map.96 = (f32[16,256,256]{2,1,0:T(8,128)}, f32[4,32,256]{2,1,0:T(8,128)}) custom-call(f32[16,10]{1,0:T(8,128)} %coeff_s.1, bf16[6,256,256]{2,1,0:T(8,128)(2,1)} %get-tuple-element.8.fmat_hbm, f32[6,8,128]{2,1,0:T(8,128)} %constant.5.clone.back_hbm, f32[2,4096,128]{2,1,0:T(8,128)} %get-tuple-element.9.warp_hbm, ...), custom_call_target="tpu_custom_call" | custom-call | tf_op jit(solution)/shard_map/pallas_call | solution.py:745
